TPU v7x, 32 devices: a whole 2x2x4 slice. The times are simulated.
32 devices in a mesh: out: 4 (over x, core), in: 8 (over z, y).
Axes of the slice: x: 2, y: 2, z: 4, core: 2. Of those that a mesh axis runs over, the one named last changes fastest.
Arguments:
- kernel_weights: bfloat16 [2, 4096, 8192], P(None, 'out', 'in'), may hold values from -0.0625 to 0.0625
- mode_field: bfloat16 [8192, 1024], P('in', 'out'), may hold values from -6 to 6
- diff_blocks: bfloat16 [2, 4096, 1024], P(None, 'out', 'in'), may hold values from -6 to 6
- block_table: int32 [4, 8], replicated, may hold values from 0 to 3, as said below
Outputs:
- gain: bfloat16 [4096, 1024], P('out', 'in')
Inputs may be any that keep to these rules, and one draw needn't show every extreme that they name: `block_table`: in every column the entries are 0 to 3, each once.
All inputs are finite; a program needn't handle non-finite values.
Results may differ from a plain program's by a relative error of at most 0.001.
Values may be sent and summed in bfloat16 or wider, within the bound.
No kernel may reach another device: no remote copies, remote signals or barrier semaphores. Data moves between devices by JAX's collectives and lax.ppermute only.
A program may use at most 64 MiB of HBM per device.

v0:
```python
import functools
import math

import jax
import jax.numpy as jnp
from jax import lax
from jax.experimental import pallas as pl
from jax.experimental.pallas import tpu as pltpu
from jax.sharding import PartitionSpec as P

PAIR = 2
TOP = 32767.0
GROUPS = 4
MERGE_COST = 100000
KERNEL_MEMORY = 24 << 20
LANES = 128


def routed_shards(kernel_weights, mode_field, diff_blocks, block_table):
    out_index = lax.axis_index("out")
    tile_rows = kernel_weights.shape[1]
    term_count = kernel_weights.shape[0]
    own_cells = diff_blocks.shape[2]
    needed_row = block_table[out_index]
    whole_field = lax.all_gather(mode_field, "out", axis=1, tiled=True)
    every_block = lax.all_gather(diff_blocks, "out", axis=1, tiled=True)
    block_count = every_block.shape[1] // tile_rows
    every_block = every_block.reshape(term_count, block_count, tile_rows, own_cells)
    arranged = jnp.take(every_block, needed_row, axis=1)
    routed = lax.all_to_all(arranged, "in", split_axis=1, concat_axis=3, tiled=True)
    partial_value = jnp.zeros((tile_rows, whole_field.shape[1]), jnp.float32)
    for term_index in range(term_count):
        product = jnp.dot(kernel_weights[term_index], whole_field, preferred_element_type=jnp.float32)
        partial_value = partial_value + routed[term_index, 0].astype(jnp.float32) * product
    summed = lax.psum_scatter(partial_value, "in", scatter_dimension=1, tiled=True)
    return summed.astype(jnp.bfloat16)


def encode(values):
    largest = jnp.maximum(jnp.max(jnp.abs(values), axis=0, keepdims=True), 1e-30)
    exponent = jnp.floor(jnp.log2(largest)) + 1.0
    share = values * (jnp.exp2(-exponent) * (TOP * TOP))
    root = share * lax.rsqrt(jnp.abs(share) + 1e-9)
    return jnp.round(root).astype(jnp.int32), exponent.astype(jnp.int32)


def pack(high, low):
    return (high << 16) | (low & 0xFFFF)


def decode(codes, exponent):
    root = codes.astype(jnp.float32)
    return root * jnp.abs(root) * (jnp.exp2(exponent.astype(jnp.float32)) * (1.0 / (TOP * TOP)))


def unpack_high(packed, exponent):
    return decode(packed >> 16, exponent)


def unpack_low(packed, exponent):
    return decode((packed << 16) >> 16, exponent)


def position(index, out_index, chips):
    crossed = jnp.where(index % PAIR != out_index % PAIR, chips, 0)
    return crossed + (out_index // PAIR - index // PAIR + chips) % chips


def choose(index, refs, *at):
    value = refs[0][at]
    for place in range(1, len(refs)):
        value = jnp.where(index == place, refs[place][at], value)
    return value


def near(value):
    return pltpu.with_memory_space_constraint(value, pltpu.VMEM)


def kernel_call(kernel, name, inputs, in_table, outputs, scratch, flops, transcendentals):
    moved = sum(math.prod(array.shape) * jnp.dtype(array.dtype).itemsize for array in [*inputs, *outputs])
    memory = pl.BlockSpec(memory_space=pltpu.VMEM)
    return pl.pallas_call(
        kernel,
        name=name,
        out_shape=outputs,
        in_specs=[pl.BlockSpec(memory_space=pltpu.SMEM)] * in_table + [memory] * (len(inputs) - in_table),
        out_specs=[memory] * len(outputs),
        scratch_shapes=scratch,
        compiler_params=pltpu.CompilerParams(vmem_limit_bytes=KERNEL_MEMORY),
        cost_estimate=pl.CostEstimate(flops=flops, bytes_accessed=moved, transcendentals=transcendentals),
    )(*inputs)


def load_kernel(*refs):
    count = len(refs) // 2
    for source, place in zip(refs[:count], refs[count:]):
        place[...] = source[...]


def load(arrays):
    return kernel_call(
        load_kernel, "load", [near(array) for array in arrays], 0,
        [pltpu.VMEM(array.shape, array.dtype) for array in arrays], [], 0, 0,
    )


def multiply_kernel(shift, columns, weights, *refs):
    *fields, kept, sent, field = refs
    terms, total, _ = weights.shape
    rows = total // GROUPS
    half = kept.shape[2]
    in_index = lax.axis_index("in")
    target = (in_index // PAIR - shift + columns) % columns
    source = position(target, lax.axis_index("out"), len(fields) // PAIR)
    side = in_index % PAIR

    for place, ref in enumerate(fields):
        for first in range(PAIR):
            @pl.when((source == place) & (side == first))
            def _():
                field[:, :half] = ref[:, first * half:(first + 1) * half]
                field[:, half:] = ref[:, (1 - first) * half:(2 - first) * half]

    for group in range(GROUPS):
        chosen = slice(group * rows, (group + 1) * rows)
        codes = []
        for term in range(terms):
            product = jnp.dot(weights[term, chosen], field[...], preferred_element_type=jnp.float32)
            kept[term, chosen] = product[:, :half]
            code, exponent = encode(product[:, half:])
            codes.append(code)
            place = total + term * GROUPS + group
            sent[place:place + 1, :] = exponent
        sent[chosen, :] = pack(*codes)


def multiply(shift, columns, weights, fields):
    terms, rows, depth = weights.shape
    width = fields[0].shape[1]
    half = width // PAIR
    return kernel_call(
        functools.partial(multiply_kernel, shift, columns),
        "products",
        [weights, *fields],
        0,
        [
            pltpu.VMEM((terms, rows, half), jnp.float32),
            pltpu.VMEM((rows + terms * GROUPS, half), jnp.int32),
        ],
        [pltpu.VMEM((depth, width), jnp.bfloat16)],
        2 * terms * rows * depth * width,
        rows * half * terms,
    )


def wanted_blocks(table, chips):
    out_index, in_index = lax.axis_index("out"), lax.axis_index("in")
    column, side = in_index // PAIR, in_index % PAIR
    return [position(table[out_index, column * PAIR + which], out_index, chips) for which in (side, 1 - side)]


def blocks_times_products(wanted, kept, received, pieces, rows, total):
    packed = received[rows, :]
    scale = total + rows.start // (total // GROUPS)
    mine = [kept[0, rows], kept[1, rows]]
    other = [
        unpack_high(packed, received[scale:scale + 1, :]),
        unpack_low(packed, received[scale + GROUPS:scale + GROUPS + 1, :]),
    ]
    value = None
    for index, products in zip(wanted, (mine, other)):
        for term, product in enumerate(products):
            chosen = choose(index, pieces, term, rows).astype(jnp.float32)
            value = chosen * product if value is None else value + chosen * product
    return value


def row_ranges(total):
    half = total // PAIR
    step = half // GROUPS
    return [
        [slice(part * half + group * step, part * half + (group + 1) * step) for part in range(PAIR)]
        for group in range(GROUPS)
    ]


def partial_kernel(table, kept, received, *refs):
    *pieces, sent = refs
    total = kept.shape[1]
    wanted = wanted_blocks(table, len(pieces) // PAIR)
    for group, parts in enumerate(row_ranges(total)):
        codes = []
        for part, rows in enumerate(parts):
            code, exponent = encode(blocks_times_products(wanted, kept, received, pieces, rows, total))
            codes.append(code)
            place = total // PAIR + part * GROUPS + group
            sent[place:place + 1, :] = exponent
        sent[parts[0], :] = pack(*codes)


def merge_kernel(*refs):
    *coming, merged = refs
    total = merged.shape[0]
    for group, parts in enumerate(row_ranges(total)):
        for part, (rows, unpack) in enumerate(zip(parts, (unpack_high, unpack_low))):
            place = total // PAIR + part * GROUPS + group
            values = [unpack(ref[parts[0], :], ref[place:place + 1, :]) for ref in coming]
            merged[rows, :] = functools.reduce(jnp.add, values)


def own_kernel(table, kept, received, merged, *refs):
    *pieces, result = refs
    total = kept.shape[1]
    wanted = wanted_blocks(table, len(pieces) // PAIR)
    for parts in row_ranges(total):
        for rows in parts:
            result[rows, :] = merged[rows, :] + blocks_times_products(wanted, kept, received, pieces, rows, total)


def final_kernel(own, last, gain):
    total = own.shape[0]
    for group, parts in enumerate(row_ranges(total)):
        for part, (rows, unpack) in enumerate(zip(parts, (unpack_high, unpack_low))):
            place = total // PAIR + part * GROUPS + group
            value = own[rows, :] + unpack(last[parts[0], :], last[place:place + 1, :])
            gain[rows, :] = value.astype(gain.dtype)


def partial_sums(table, kept, received, pieces):
    terms, rows, cells = kept.shape
    shape = (rows // PAIR + PAIR * GROUPS, cells)
    return kernel_call(
        partial_kernel, "partial_sums", [table, kept, received, *pieces], 1,
        [pltpu.VMEM(shape, jnp.int32)], [], 8 * terms * rows * cells, rows * cells,
    )[0]


def merged_sums(coming, rows):
    cells = coming[0].shape[1]
    return kernel_call(
        merge_kernel, "merged_sums", coming, 0,
        [pltpu.VMEM((rows, cells), jnp.float32)], [], MERGE_COST * rows * cells, 0,
    )[0]


def own_sums(table, kept, received, merged, pieces):
    terms, rows, cells = kept.shape
    return kernel_call(
        own_kernel, "own_sums", [table, kept, received, merged, *pieces], 1,
        [pltpu.VMEM((rows, cells), jnp.float32)], [], 8 * terms * rows * cells, 0,
    )[0]


def final_sums(own, last):
    rows, cells = own.shape
    return kernel_call(
        final_kernel, "final_sums", [own, last], 0,
        [jax.ShapeDtypeStruct((rows, cells), jnp.bfloat16)], [], 4 * rows * cells, 0,
    )[0]


def after(value, *earlier):
    return lax.optimization_barrier((value, *earlier))[0]


def gathered_shards(out_count, in_count, kernel_weights, mode_field, diff_blocks, block_table):
    columns = in_count // PAIR

    def across_cores(value):
        return lax.ppermute(value, "out", [(r, r ^ 1) for r in range(out_count)])

    def along_chips(value):
        return lax.ppermute(value, "out", [(r, (r + PAIR) % out_count) for r in range(out_count)])

    def across_sides(value):
        return lax.ppermute(value, "in", [(s, s ^ 1) for s in range(in_count)])

    def along_columns(value, shift):
        return lax.ppermute(value, "in", [(s, (s + PAIR * shift) % in_count) for s in range(in_count)])

    order = list(range(1, columns)) + [0]
    weights, own_field, own_blocks = load([kernel_weights, mode_field, diff_blocks])
    far_field = after(along_chips(mode_field), weights)
    fields = [own_field] + [near(field) for field in (far_field, across_cores(mode_field), across_cores(far_field))]

    rings = [diff_blocks]
    for step in range(1, columns):
        rings.append(along_columns(rings[-1], 1))
    kept, sent = {}, {}
    for step in order:
        kept[step], sent[step] = multiply(step, columns, weights, fields)
    core_own = across_cores(diff_blocks)
    far_own = along_chips(after(diff_blocks, far_field))
    far, pieces = [far_own], {}
    for place, step in enumerate(order[:-1]):
        earlier = [[far_field], [*sent.values(), core_own, far[-1]]][place] if place < 2 else far[-1:]
        far.append(along_chips(after(rings[step], *earlier)))
        pieces[step] = [near(rings[step]), near(far[-1])]
        pieces[step] += [near(across_cores(piece)) for piece in (rings[step], far[-1])]

    received, coming = {}, []

    def send_sums(place):
        step = order[place]
        ready = after(kept[step], *(coming[-1:] if place < columns - 2 else []))
        partial = partial_sums(block_table, ready, received[step], pieces[step])
        coming.append(near(along_columns(partial, -step)))
        return partial

    for place, step in enumerate(order):
        earlier = [received[order[place - 1]]] if place > 0 else []
        if place > 1:
            earlier.append(send_sums(place - 2))
        received[step] = near(across_sides(after(sent[step], *earlier)))
    latest = send_sums(columns - 2)
    pieces[0] = [own_blocks, near(far_own), near(core_own), near(across_cores(after(far_own, latest)))]
    merged = near(merged_sums(coming[:-1], kernel_weights.shape[1]))
    own = near(own_sums(block_table, kept[0], received[0], merged, pieces[0]))
    return final_sums(own, coming[-1])


def solution(mesh):
    out_count, in_count = mesh.shape["out"], mesh.shape["in"]
    in_specs = (P(None, "out", "in"), P("in", "out"), P(None, "out", "in"), P())
    out_specs = P("out", "in")

    def shards(kernel_weights, mode_field, diff_blocks, block_table):
        own_cells = diff_blocks.shape[2]
        gather = (
            kernel_weights.shape[0] == PAIR
            and own_cells % LANES == 0
            and mode_field.shape[1] == PAIR * own_cells
            and out_count == PAIR * PAIR
            and in_count == PAIR * out_count
        )
        if gather:
            return gathered_shards(out_count, in_count, kernel_weights, mode_field, diff_blocks, block_table)
        return routed_shards(kernel_weights, mode_field, diff_blocks, block_table)

    return jax.shard_map(shards, mesh=mesh, in_specs=in_specs, out_specs=out_specs, check_vma=False)
```

profile of v0, /device:TPU:0, one launch (start us, length us, event | category | flops | bytes accessed | tf_op | source)
XLA Modules:
  0.0 84.2 jit_solution(9560778002939145140)
XLA Ops:
  0.0 2.9 %collective-permute-start = (bf16[1024,256]{1,0:T(8,128)(2,1)}, bf16[1024,256]{1,0:T(8,128)(2,1)S(1)}, u32[]{:S(2)}, u32[]{:S(2)}) collective-permute-start(bf16[1024,256]{1,0:T(8,128)(2,1)} %refs_1_.1), channel_id=1, source_target_pairs={{0,16},{8,24},{16,0},{24,8},{1,17},{9,25},{17,1},{25,9},{2,18},{10... | collective-permute-start | bytes 1572872 | tf_op jit(solution)/shard_map/ppermute | solution.py:274
  2.9 1.6 %collective-permute-start.5 = (bf16[2,1024,128]{2,1,0:T(8,128)(2,1)}, bf16[2,1024,128]{2,1,0:T(8,128)(2,1)S(1)}, u32[]{:S(2)}, u32[]{:S(2)}) collective-permute-start(bf16[2,1024,128]{2,1,0:T(8,128)(2,1)} %refs_2_.1), channel_id=1, source_target_pairs={{0,2},{1,3},{2,4},{3,5},{4,6},{5,7},{6,0},{7,1},{8,10},{9,11},{10,... | collective-permute-start | bytes 1572872 | tf_op jit(solution)/shard_map/ppermute | solution.py:280
  4.5 2.2 %copy-done = bf16[2,1024,1024]{2,1,0:T(8,128)(2,1)S(1)} copy-done((bf16[2,1024,1024]{2,1,0:T(8,128)(2,1)S(1)}, bf16[2,1024,1024]{2,1,0:T(8,128)(2,1)}, u32[]{:S(2)}) %copy-start) | copy-done | bytes 4194328
  9.1 5.9 %collective-permute-done.refs_1_ = bf16[1024,256]{1,0:T(8,128)(2,1)S(1)} collective-permute-done((bf16[1024,256]{1,0:T(8,128)(2,1)}, bf16[1024,256]{1,0:T(8,128)(2,1)S(1)}, u32[]{:S(2)}, u32[]{:S(2)}) %collective-permute-start) | collective-permute-done | bytes 524320 | tf_op jit(solution)/shard_map/ppermute | solution.py:274
  15.6 2.8 %collective-permute-done.5.refs_0_ = bf16[2,1024,128]{2,1,0:T(8,128)(2,1)S(1)} collective-permute-done((bf16[2,1024,128]{2,1,0:T(8,128)(2,1)}, bf16[2,1024,128]{2,1,0:T(8,128)(2,1)S(1)}, u32[]{:S(2)}, u32[]{:S(2)}) %collective-permute-start.5) | collective-permute-done | bytes 524320 | tf_op jit(solution)/shard_map/ppermute | solution.py:280
  18.9 1.6 %products.7 = (f32[2,1024,128]{2,1,0:T(8,128)S(1)}, s32[1032,128]{1,0:T(8,128)S(1)}) custom-call(bf16[2,1024,1024]{2,1,0:T(8,128)(2,1)S(1)} %get-tuple-element.26.weights, bf16[1024,256]{1,0:T(8,128)(2,1)S(1)} %get-tuple-element.27.refs_0_, bf16[1024,256]{1,0:T(8,128)(2,1)S(1)} %collective-permute-done.refs_1_, ...), custom_call_target="tpu_custom_call" | custom-call | flops 1073741824 | bytes 7868416 | tf_op jit(solution)/shard_map/products/pallas_call | solution.py:83
  20.5 1.6 %collective-permute-start.3 = (s32[1032,128]{1,0:T(8,128)S(1)}, s32[1032,128]{1,0:T(8,128)S(1)}, u32[]{:S(2)}, u32[]{:S(2)}) collective-permute-start(s32[1032,128]{1,0:T(8,128)S(1)} %get-tuple-element.33), channel_id=1, source_target_pairs={{0,1},{1,0},{2,3},{3,2},{4,5},{5,4},{6,7},{7,6},{8,9},{9,8},{10,11... | collective-permute-start | bytes 1585160 | tf_op jit(solution)/shard_map/ppermute | solution.py:277
  22.1 1.5 %products.4 = (f32[2,1024,128]{2,1,0:T(8,128)S(1)}, s32[1032,128]{1,0:T(8,128)S(1)}) custom-call(bf16[2,1024,1024]{2,1,0:T(8,128)(2,1)S(1)} %get-tuple-element.26.weights, bf16[1024,256]{1,0:T(8,128)(2,1)S(1)} %get-tuple-element.27.refs_0_, bf16[1024,256]{1,0:T(8,128)(2,1)S(1)} %collective-permute-done.refs_1_, ...), custom_call_target="tpu_custom_call" | custom-call | flops 1073741824 | bytes 7868416 | tf_op jit(solution)/shard_map/products/pallas_call | solution.py:83
  23.7 1.6 %products.5 = (f32[2,1024,128]{2,1,0:T(8,128)S(1)}, s32[1032,128]{1,0:T(8,128)S(1)}) custom-call(bf16[2,1024,1024]{2,1,0:T(8,128)(2,1)S(1)} %get-tuple-element.26.weights, bf16[1024,256]{1,0:T(8,128)(2,1)S(1)} %get-tuple-element.27.refs_0_, bf16[1024,256]{1,0:T(8,128)(2,1)S(1)} %collective-permute-done.refs_1_, ...), custom_call_target="tpu_custom_call" | custom-call | flops 1073741824 | bytes 7868416 | tf_op jit(solution)/shard_map/products/pallas_call | solution.py:83
  25.3 1.6 %products.6 = (f32[2,1024,128]{2,1,0:T(8,128)S(1)}, s32[1032,128]{1,0:T(8,128)S(1)}) custom-call(bf16[2,1024,1024]{2,1,0:T(8,128)(2,1)S(1)} %get-tuple-element.26.weights, bf16[1024,256]{1,0:T(8,128)(2,1)S(1)} %get-tuple-element.27.refs_0_, bf16[1024,256]{1,0:T(8,128)(2,1)S(1)} %collective-permute-done.refs_1_, ...), custom_call_target="tpu_custom_call" | custom-call | flops 1073741824 | bytes 7868416 | tf_op jit(solution)/shard_map/products/pallas_call | solution.py:83
  26.8 4.1 %collective-permute-done.6.refs_1_ = bf16[2,1024,128]{2,1,0:T(8,128)(2,1)S(1)} collective-permute-done((bf16[2,1024,128]{2,1,0:T(8,128)(2,1)S(1)}, bf16[2,1024,128]{2,1,0:T(8,128)(2,1)S(1)}, u32[]{:S(2)}, u32[]{:S(2)}) %collective-permute-start.6) | collective-permute-done | bytes 524320 | tf_op jit(solution)/shard_map/ppermute | solution.py:274
  30.9 2.3 %collective-permute-done.11.refs_0_ = bf16[2,1024,128]{2,1,0:T(8,128)(2,1)S(1)} collective-permute-done((bf16[2,1024,128]{2,1,0:T(8,128)(2,1)S(1)}, bf16[2,1024,128]{2,1,0:T(8,128)(2,1)S(1)}, u32[]{:S(2)}, u32[]{:S(2)}) %collective-permute-start.11) | collective-permute-done | bytes 524320 | tf_op jit(solution)/shard_map/ppermute | solution.py:280
  35.0 1.5 %collective-permute-start.4 = (s32[1032,128]{1,0:T(8,128)S(1)}, s32[1032,128]{1,0:T(8,128)S(1)}, u32[]{:S(2)}, u32[]{:S(2)}) collective-permute-start(s32[1032,128]{1,0:T(8,128)S(1)} %get-tuple-element.34), channel_id=1, source_target_pairs={{0,1},{1,0},{2,3},{3,2},{4,5},{5,4},{6,7},{7,6},{8,9},{9,8},{10,11... | collective-permute-start | bytes 1585160 | tf_op jit(solution)/shard_map/ppermute | solution.py:277
  36.5 8.3 %collective-permute-done.13.refs_1_ = bf16[2,1024,128]{2,1,0:T(8,128)(2,1)S(1)} collective-permute-done((bf16[2,1024,128]{2,1,0:T(8,128)(2,1)S(1)}, bf16[2,1024,128]{2,1,0:T(8,128)(2,1)S(1)}, u32[]{:S(2)}, u32[]{:S(2)}) %collective-permute-start.13) | collective-permute-done | bytes 524320 | tf_op jit(solution)/shard_map/ppermute | solution.py:274
  44.8 2.5 %collective-permute-done.19.refs_0_ = bf16[2,1024,128]{2,1,0:T(8,128)(2,1)S(1)} collective-permute-done((bf16[2,1024,128]{2,1,0:T(8,128)(2,1)S(1)}, bf16[2,1024,128]{2,1,0:T(8,128)(2,1)S(1)}, u32[]{:S(2)}, u32[]{:S(2)}) %collective-permute-start.19) | collective-permute-done | bytes 524320 | tf_op jit(solution)/shard_map/ppermute | solution.py:280
  48.4 1.5 %partial_sums.3 = s32[520,128]{1,0:T(8,128)S(1)} custom-call(s32[4,8]{1,0:T(4,128)S(1)} %copy-done.2, f32[2,1024,128]{2,1,0:T(8,128)S(1)} %get-tuple-element.35.kept, s32[1032,128]{1,0:T(8,128)S(1)} %collective-permute-done.3.received, bf16[2,1024,128]{2,1,0:T(8,128)(2,1)S(1)} %collective-permute-done.5.refs_0_, ...), custom_call_target="tpu_custom_call" | custom-call | flops 2097152 | bytes 3940480 | tf_op jit(solution)/shard_map/partial_sums/pallas_call | solution.py:83
  50.6 1.5 %collective-permute-start.9 = (s32[1032,128]{1,0:T(8,128)S(1)}, s32[1032,128]{1,0:T(8,128)S(1)}, u32[]{:S(2)}, u32[]{:S(2)}) collective-permute-start(s32[1032,128]{1,0:T(8,128)S(1)} %get-tuple-element.37), channel_id=1, source_target_pairs={{0,1},{1,0},{2,3},{3,2},{4,5},{5,4},{6,7},{7,6},{8,9},{9,8},{10,11... | collective-permute-start | bytes 1585160 | tf_op jit(solution)/shard_map/ppermute | solution.py:277
  52.4 6.8 %collective-permute-done.20.refs_1_ = bf16[2,1024,128]{2,1,0:T(8,128)(2,1)S(1)} collective-permute-done((bf16[2,1024,128]{2,1,0:T(8,128)(2,1)S(1)}, bf16[2,1024,128]{2,1,0:T(8,128)(2,1)S(1)}, u32[]{:S(2)}, u32[]{:S(2)}) %collective-permute-start.20) | collective-permute-done | bytes 524320 | tf_op jit(solution)/shard_map/ppermute | solution.py:274
  60.2 1.5 %partial_sums.4 = s32[520,128]{1,0:T(8,128)S(1)} custom-call(s32[4,8]{1,0:T(4,128)S(1)} %copy-done.2, f32[2,1024,128]{2,1,0:T(8,128)S(1)} %get-tuple-element.39.kept, s32[1032,128]{1,0:T(8,128)S(1)} %collective-permute-done.4.received, bf16[2,1024,128]{2,1,0:T(8,128)(2,1)S(1)} %collective-permute-done.11.refs_0_, ...), custom_call_target="tpu_custom_call" | custom-call | flops 2097152 | bytes 3940480 | tf_op jit(solution)/shard_map/partial_sums/pallas_call | solution.py:83
  62.7 2.4 %collective-permute-done.9.received = s32[1032,128]{1,0:T(8,128)S(1)} collective-permute-done((s32[1032,128]{1,0:T(8,128)S(1)}, s32[1032,128]{1,0:T(8,128)S(1)}, u32[]{:S(2)}, u32[]{:S(2)}) %collective-permute-start.9) | collective-permute-done | bytes 528416 | tf_op jit(solution)/shard_map/ppermute | solution.py:277
  65.1 1.5 %collective-permute-start.16 = (s32[1032,128]{1,0:T(8,128)S(1)}, s32[1032,128]{1,0:T(8,128)S(1)}, u32[]{:S(2)}, u32[]{:S(2)}) collective-permute-start(s32[1032,128]{1,0:T(8,128)S(1)} %get-tuple-element.41), channel_id=1, source_target_pairs={{0,1},{1,0},{2,3},{3,2},{4,5},{5,4},{6,7},{7,6},{8,9},{9,8},{10,11... | collective-permute-start | bytes 1585160 | tf_op jit(solution)/shard_map/ppermute | solution.py:277
  66.6 1.5 %partial_sums.5 = s32[520,128]{1,0:T(8,128)S(1)} custom-call(s32[4,8]{1,0:T(4,128)S(1)} %copy-done.2, f32[2,1024,128]{2,1,0:T(8,128)S(1)} %get-tuple-element.44.kept, s32[1032,128]{1,0:T(8,128)S(1)} %collective-permute-done.9.received, bf16[2,1024,128]{2,1,0:T(8,128)(2,1)S(1)} %collective-permute-done.19.refs_0_, ...), custom_call_target="tpu_custom_call" | custom-call | flops 2097152 | bytes 3940480 | tf_op jit(solution)/shard_map/partial_sums/pallas_call | solution.py:83
  69.1 4.6 %collective-permute-done.18.refs_1_ = bf16[2,1024,128]{2,1,0:T(8,128)(2,1)S(1)} collective-permute-done((bf16[2,1024,128]{2,1,0:T(8,128)(2,1)}, bf16[2,1024,128]{2,1,0:T(8,128)(2,1)S(1)}, u32[]{:S(2)}, u32[]{:S(2)}) %collective-permute-start.18) | collective-permute-done | bytes 524320 | tf_op jit(solution)/shard_map/ppermute | solution.py:274
  73.7 8.2 %collective-permute-done.17.refs_1_ = s32[520,128]{1,0:T(8,128)S(1)} collective-permute-done((s32[520,128]{1,0:T(8,128)S(1)}, s32[520,128]{1,0:T(8,128)S(1)}, u32[]{:S(2)}, u32[]{:S(2)}) %collective-permute-start.17) | collective-permute-done | bytes 266272 | tf_op jit(solution)/shard_map/ppermute | solution.py:280
  (43 shorter events, 12.6 us)
Async XLA Ops:
  0.0 15.1 %collective-permute-start = (bf16[1024,256]{1,0:T(8,128)(2,1)}, bf16[1024,256]{1,0:T(8,128)(2,1)S(1)}, u32[]{:S(2)}, u32[]{:S(2)}) collective-permute-start(bf16[1024,256]{1,0:T(8,128)(2,1)} %refs_1_.1), channel_id=1, source_target_pairs={{0,16},{8,24},{16,0},{24,8},{1,17},{9,25},{17,1},{25,9},{2,18},{10... | collective-permute-start | bytes 1572872 | tf_op jit(solution)/shard_map/ppermute | solution.py:274
  2.9 15.5 %collective-permute-start.5 = (bf16[2,1024,128]{2,1,0:T(8,128)(2,1)}, bf16[2,1024,128]{2,1,0:T(8,128)(2,1)S(1)}, u32[]{:S(2)}, u32[]{:S(2)}) collective-permute-start(bf16[2,1024,128]{2,1,0:T(8,128)(2,1)} %refs_2_.1), channel_id=1, source_target_pairs={{0,2},{1,3},{2,4},{3,5},{4,6},{5,7},{6,0},{7,1},{8,10},{9,11},{10,... | collective-permute-start | bytes 1572872 | tf_op jit(solution)/shard_map/ppermute | solution.py:280
  4.5 14.4 %collective-permute-start.1 = (bf16[1024,256]{1,0:T(8,128)(2,1)}, bf16[1024,256]{1,0:T(8,128)(2,1)S(1)}, u32[]{:S(2)}, u32[]{:S(2)}) collective-permute-start(bf16[1024,256]{1,0:T(8,128)(2,1)} %refs_1_.1), channel_id=1, source_target_pairs={{0,8},{8,0},{16,24},{24,16},{1,9},{9,1},{17,25},{25,17},{2,10},{10... | collective-permute-start | bytes 1572872 | tf_op jit(solution)/shard_map/ppermute | solution.py:271
  15.1 11.8 %collective-permute-start.12 = (bf16[2,1024,128]{2,1,0:T(8,128)(2,1)}, bf16[2,1024,128]{2,1,0:T(8,128)(2,1)S(1)}, u32[]{:S(2)}, u32[]{:S(2)}) collective-permute-start(bf16[2,1024,128]{2,1,0:T(8,128)(2,1)} %refs_2_.1), channel_id=1, source_target_pairs={{0,8},{8,0},{16,24},{24,16},{1,9},{9,1},{17,25},{25,17},{2,10},{10... | collective-permute-start | bytes 1572872 | tf_op jit(solution)/shard_map/ppermute | solution.py:271
  18.4 12.5 %collective-permute-start.6 = (bf16[2,1024,128]{2,1,0:T(8,128)(2,1)S(1)}, bf16[2,1024,128]{2,1,0:T(8,128)(2,1)S(1)}, u32[]{:S(2)}, u32[]{:S(2)}) collective-permute-start(bf16[2,1024,128]{2,1,0:T(8,128)(2,1)S(1)} %collective-permute-done.5.refs_0_), channel_id=1, source_target_pairs={{0,16},{8,24},{16,0},{24,8},{1,17},{9,25},{17,1},{25,9},{2,18},{10... | collective-permute-start | bytes 1572872 | tf_op jit(solution)/shard_map/ppermute | solution.py:274
  18.9 14.3 %collective-permute-start.11 = (bf16[2,1024,128]{2,1,0:T(8,128)(2,1)S(1)}, bf16[2,1024,128]{2,1,0:T(8,128)(2,1)S(1)}, u32[]{:S(2)}, u32[]{:S(2)}) collective-permute-start(bf16[2,1024,128]{2,1,0:T(8,128)(2,1)S(1)} %collective-permute-done.5.refs_0_), channel_id=1, source_target_pairs={{0,2},{1,3},{2,4},{3,5},{4,6},{5,7},{6,0},{7,1},{8,10},{9,11},{10,... | collective-permute-start | bytes 1572872 | tf_op jit(solution)/shard_map/ppermute | solution.py:280
  20.5 14.5 %collective-permute-start.3 = (s32[1032,128]{1,0:T(8,128)S(1)}, s32[1032,128]{1,0:T(8,128)S(1)}, u32[]{:S(2)}, u32[]{:S(2)}) collective-permute-start(s32[1032,128]{1,0:T(8,128)S(1)} %get-tuple-element.33), channel_id=1, source_target_pairs={{0,1},{1,0},{2,3},{3,2},{4,5},{5,4},{6,7},{7,6},{8,9},{9,8},{10,11... | collective-permute-start | bytes 1585160 | tf_op jit(solution)/shard_map/ppermute | solution.py:277
  33.2 11.6 %collective-permute-start.13 = (bf16[2,1024,128]{2,1,0:T(8,128)(2,1)S(1)}, bf16[2,1024,128]{2,1,0:T(8,128)(2,1)S(1)}, u32[]{:S(2)}, u32[]{:S(2)}) collective-permute-start(bf16[2,1024,128]{2,1,0:T(8,128)(2,1)S(1)} %collective-permute-done.11.refs_0_), channel_id=1, source_target_pairs={{0,16},{8,24},{16,0},{24,8},{1,17},{9,25},{17,1},{25,9},{2,18},{10... | collective-permute-start | bytes 1572872 | tf_op jit(solution)/shard_map/ppermute | solution.py:274
  34.5 12.9 %collective-permute-start.19 = (bf16[2,1024,128]{2,1,0:T(8,128)(2,1)S(1)}, bf16[2,1024,128]{2,1,0:T(8,128)(2,1)S(1)}, u32[]{:S(2)}, u32[]{:S(2)}) collective-permute-start(bf16[2,1024,128]{2,1,0:T(8,128)(2,1)S(1)} %collective-permute-done.11.refs_0_), channel_id=1, source_target_pairs={{0,2},{1,3},{2,4},{3,5},{4,6},{5,7},{6,0},{7,1},{8,10},{9,11},{10,... | collective-permute-start | bytes 1572872 | tf_op jit(solution)/shard_map/ppermute | solution.py:280
  34.5 13.9 %collective-permute-start.7 = (bf16[2,1024,128]{2,1,0:T(8,128)(2,1)S(1)}, bf16[2,1024,128]{2,1,0:T(8,128)(2,1)S(1)}, u32[]{:S(2)}, u32[]{:S(2)}) collective-permute-start(bf16[2,1024,128]{2,1,0:T(8,128)(2,1)S(1)} %collective-permute-done.5.refs_0_), channel_id=1, source_target_pairs={{0,8},{8,0},{16,24},{24,16},{1,9},{9,1},{17,25},{25,17},{2,10},{10... | collective-permute-start | bytes 1572872 | tf_op jit(solution)/shard_map/ppermute | solution.py:271
  34.5 13.9 %collective-permute-start.8 = (bf16[2,1024,128]{2,1,0:T(8,128)(2,1)S(1)}, bf16[2,1024,128]{2,1,0:T(8,128)(2,1)S(1)}, u32[]{:S(2)}, u32[]{:S(2)}) collective-permute-start(bf16[2,1024,128]{2,1,0:T(8,128)(2,1)S(1)} %collective-permute-done.6.refs_1_), channel_id=1, source_target_pairs={{0,8},{8,0},{16,24},{24,16},{1,9},{9,1},{17,25},{25,17},{2,10},{10... | collective-permute-start | bytes 1572872 | tf_op jit(solution)/shard_map/ppermute | solution.py:271
  35.0 15.6 %collective-permute-start.4 = (s32[1032,128]{1,0:T(8,128)S(1)}, s32[1032,128]{1,0:T(8,128)S(1)}, u32[]{:S(2)}, u32[]{:S(2)}) collective-permute-start(s32[1032,128]{1,0:T(8,128)S(1)} %get-tuple-element.34), channel_id=1, source_target_pairs={{0,1},{1,0},{2,3},{3,2},{4,5},{5,4},{6,7},{7,6},{8,9},{9,8},{10,11... | collective-permute-start | bytes 1585160 | tf_op jit(solution)/shard_map/ppermute | solution.py:277
  44.8 7.3 %collective-permute-start.14 = (bf16[2,1024,128]{2,1,0:T(8,128)(2,1)S(1)}, bf16[2,1024,128]{2,1,0:T(8,128)(2,1)S(1)}, u32[]{:S(2)}, u32[]{:S(2)}) collective-permute-start(bf16[2,1024,128]{2,1,0:T(8,128)(2,1)S(1)} %collective-permute-done.11.refs_0_), channel_id=1, source_target_pairs={{0,8},{8,0},{16,24},{24,16},{1,9},{9,1},{17,25},{25,17},{2,10},{10... | collective-permute-start | bytes 1572872 | tf_op jit(solution)/shard_map/ppermute | solution.py:271
  47.3 11.8 %collective-permute-start.20 = (bf16[2,1024,128]{2,1,0:T(8,128)(2,1)S(1)}, bf16[2,1024,128]{2,1,0:T(8,128)(2,1)S(1)}, u32[]{:S(2)}, u32[]{:S(2)}) collective-permute-start(bf16[2,1024,128]{2,1,0:T(8,128)(2,1)S(1)} %collective-permute-done.19.refs_0_), channel_id=1, source_target_pairs={{0,16},{8,24},{16,0},{24,8},{1,17},{9,25},{17,1},{25,9},{2,18},{10... | collective-permute-start | bytes 1572872 | tf_op jit(solution)/shard_map/ppermute | solution.py:274
  49.9 9.3 %collective-permute-start.10 = (s32[520,128]{1,0:T(8,128)S(1)}, s32[520,128]{1,0:T(8,128)S(1)}, u32[]{:S(2)}, u32[]{:S(2)}) collective-permute-start(s32[520,128]{1,0:T(8,128)S(1)} %partial_sums.3), channel_id=1, source_target_pairs={{0,6},{1,7},{2,0},{3,1},{4,2},{5,3},{6,4},{7,5},{8,14},{9,15},{10,... | collective-permute-start | bytes 798728 | tf_op jit(solution)/shard_map/ppermute | solution.py:280
  50.6 9.5 %collective-permute-start.15 = (bf16[2,1024,128]{2,1,0:T(8,128)(2,1)S(1)}, bf16[2,1024,128]{2,1,0:T(8,128)(2,1)S(1)}, u32[]{:S(2)}, u32[]{:S(2)}) collective-permute-start(bf16[2,1024,128]{2,1,0:T(8,128)(2,1)S(1)} %collective-permute-done.13.refs_1_), channel_id=1, source_target_pairs={{0,8},{8,0},{16,24},{24,16},{1,9},{9,1},{17,25},{25,17},{2,10},{10... | collective-permute-start | bytes 1572872 | tf_op jit(solution)/shard_map/ppermute | solution.py:271
  50.6 14.4 %collective-permute-start.9 = (s32[1032,128]{1,0:T(8,128)S(1)}, s32[1032,128]{1,0:T(8,128)S(1)}, u32[]{:S(2)}, u32[]{:S(2)}) collective-permute-start(s32[1032,128]{1,0:T(8,128)S(1)} %get-tuple-element.37), channel_id=1, source_target_pairs={{0,1},{1,0},{2,3},{3,2},{4,5},{5,4},{6,7},{7,6},{8,9},{9,8},{10,11... | collective-permute-start | bytes 1585160 | tf_op jit(solution)/shard_map/ppermute | solution.py:277
  52.2 14.4 %collective-permute-start.21 = (bf16[2,1024,128]{2,1,0:T(8,128)(2,1)S(1)}, bf16[2,1024,128]{2,1,0:T(8,128)(2,1)S(1)}, u32[]{:S(2)}, u32[]{:S(2)}) collective-permute-start(bf16[2,1024,128]{2,1,0:T(8,128)(2,1)S(1)} %collective-permute-done.19.refs_0_), channel_id=1, source_target_pairs={{0,8},{8,0},{16,24},{24,16},{1,9},{9,1},{17,25},{25,17},{2,10},{10... | collective-permute-start | bytes 1572872 | tf_op jit(solution)/shard_map/ppermute | solution.py:271
  59.2 7.4 %collective-permute-start.22 = (bf16[2,1024,128]{2,1,0:T(8,128)(2,1)S(1)}, bf16[2,1024,128]{2,1,0:T(8,128)(2,1)S(1)}, u32[]{:S(2)}, u32[]{:S(2)}) collective-permute-start(bf16[2,1024,128]{2,1,0:T(8,128)(2,1)S(1)} %collective-permute-done.20.refs_1_), channel_id=1, source_target_pairs={{0,8},{8,0},{16,24},{24,16},{1,9},{9,1},{17,25},{25,17},{2,10},{10... | collective-permute-start | bytes 1572872 | tf_op jit(solution)/shard_map/ppermute | solution.py:271
  59.2 14.5 %collective-permute-start.18 = (bf16[2,1024,128]{2,1,0:T(8,128)(2,1)}, bf16[2,1024,128]{2,1,0:T(8,128)(2,1)S(1)}, u32[]{:S(2)}, u32[]{:S(2)}) collective-permute-start(bf16[2,1024,128]{2,1,0:T(8,128)(2,1)} %refs_2_.1), channel_id=1, source_target_pairs={{0,16},{8,24},{16,0},{24,8},{1,17},{9,25},{17,1},{25,9},{2,18},{10... | collective-permute-start | bytes 1572872 | tf_op jit(solution)/shard_map/ppermute | solution.py:274
  61.7 20.2 %collective-permute-start.17 = (s32[520,128]{1,0:T(8,128)S(1)}, s32[520,128]{1,0:T(8,128)S(1)}, u32[]{:S(2)}, u32[]{:S(2)}) collective-permute-start(s32[520,128]{1,0:T(8,128)S(1)} %partial_sums.4), channel_id=1, source_target_pairs={{0,4},{1,5},{2,6},{3,7},{4,0},{5,1},{6,2},{7,3},{8,12},{9,13},{10,... | collective-permute-start | bytes 798728 | tf_op jit(solution)/shard_map/ppermute | solution.py:280
  65.1 17.1 %collective-permute-start.16 = (s32[1032,128]{1,0:T(8,128)S(1)}, s32[1032,128]{1,0:T(8,128)S(1)}, u32[]{:S(2)}, u32[]{:S(2)}) collective-permute-start(s32[1032,128]{1,0:T(8,128)S(1)} %get-tuple-element.41), channel_id=1, source_target_pairs={{0,1},{1,0},{2,3},{3,2},{4,5},{5,4},{6,7},{7,6},{8,9},{9,8},{10,11... | collective-permute-start | bytes 1585160 | tf_op jit(solution)/shard_map/ppermute | solution.py:277
  68.1 15.3 %collective-permute-start.24 = (s32[520,128]{1,0:T(8,128)S(1)}, s32[520,128]{1,0:T(8,128)S(1)}, u32[]{:S(2)}, u32[]{:S(2)}) collective-permute-start(s32[520,128]{1,0:T(8,128)S(1)} %partial_sums.5), channel_id=1, source_target_pairs={{0,2},{1,3},{2,4},{3,5},{4,6},{5,7},{6,0},{7,1},{8,10},{9,11},{10,... | collective-permute-start | bytes 798728 | tf_op jit(solution)/shard_map/ppermute | solution.py:280
  73.7 8.4 %collective-permute-start.23 = (bf16[2,1024,128]{2,1,0:T(8,128)(2,1)S(1)}, bf16[2,1024,128]{2,1,0:T(8,128)(2,1)S(1)}, u32[]{:S(2)}, u32[]{:S(2)}) collective-permute-start(bf16[2,1024,128]{2,1,0:T(8,128)(2,1)S(1)} %collective-permute-done.18.refs_1_), channel_id=1, source_target_pairs={{0,8},{8,0},{16,24},{24,16},{1,9},{9,1},{17,25},{25,17},{2,10},{10... | collective-permute-start | bytes 1572872 | tf_op jit(solution)/shard_map/ppermute | solution.py:271
  (4 other events, 30.2 us)
where the time goes:
time: 84.5 us; the launch traced here: 84.2 us
  waiting for transfers between devices  48 us (57%)
  starting transfers between devices  18.6 us (22%)
  Pallas kernels  14.3 us (17%)
  local copies, waits for them, and re-layouts  3.24 us (4%)
    ppermute x5, waiting for transfers between devices, along_chips(): lax.ppermute(value, 'out', [(r, (r + PAIR) % out_count) for r in range(ou...  29.7 us
    ppermute x6, waiting for transfers between devices, along_columns(): lax.ppermute(value, 'in', [(s, (s + PAIR * shift) % in_count) for s in ra...  15.8 us
    pallas_call x11, Pallas kernels, kernel_call(): pl.pallas_call(kernel, name=name, out_shape=outputs, in_specs=[pl.BlockSp...  14.3 us
    ppermute x5, starting transfers between devices, along_chips(): lax.ppermute(value, 'out', [(r, (r + PAIR) % out_count) for r in range(ou...  6.74 us
    ppermute x4, starting transfers between devices, across_sides(): return lax.ppermute(value, 'in', [(s, s ^ 1) for s in range(in_count)])  6.2 us
    ppermute x6, starting transfers between devices, along_columns(): lax.ppermute(value, 'in', [(s, (s + PAIR * shift) % in_count) for s in ra...  4.37 us
    unnamed x6, local copies, waits for them, and re-layouts  3.24 us
    ppermute x4, waiting for transfers between devices, across_sides(): return lax.ppermute(value, 'in', [(s, s ^ 1) for s in range(in_count)])  2.42 us
  transfers between devices with their start and end apart: 25, of which 10 were waited for; matrix products, arithmetic and copies ran while one was open for 0% of the time, Pallas kernels for 16%

commit v1 on v0

--- a/solution.py
+++ b/solution.py
@@ -296,13 +296,14 @@
     for place, step in enumerate(order[:-1]):
         earlier = [[far_field], [*sent.values(), core_own, far[-1]]][place] if place < 2 else far[-1:]
         far.append(along_chips(after(rings[step], *earlier)))
-        pieces[step] = [near(rings[step]), near(far[-1])]
-        pieces[step] += [near(across_cores(piece)) for piece in (rings[step], far[-1])]
 
     received, coming = {}, []
 
     def send_sums(place):
         step = order[place]
+        swapped = [received[step]] if place == 1 else []
+        pieces[step] = [near(rings[step]), near(far[place + 1]), near(across_cores(rings[step]))]
+        pieces[step].append(near(across_cores(after(far[place + 1], *swapped))))
         ready = after(kept[step], *(coming[-1:] if place < columns - 2 else []))
         partial = partial_sums(block_table, ready, received[step], pieces[step])
         coming.append(near(along_columns(partial, -step)))

time: 84.5 us -> 83.6 us (0.989)
    ppermute x5, waiting for transfers between devices: 29.7 us -> 27 us  [along_chips(): lax.ppermute(value, 'out', [(r, (r + PAIR) % out_count) for r in range(ou...]
    ppermute x4, waiting for transfers between devices: 2.42 us -> 3.59 us  [across_sides(): return lax.ppermute(value, 'in', [(s, s ^ 1) for s in range(in_count)])]
    ppermute x6, waiting for transfers between devices: 15.8 us -> 16.9 us  [along_columns(): lax.ppermute(value, 'in', [(s, (s + PAIR * shift) % in_count) for s in ra...]
    ppermute x6, starting transfers between devices: 4.37 us -> 3.46 us  [along_columns(): lax.ppermute(value, 'in', [(s, (s + PAIR * shift) % in_count) for s in ra...]
  transfers between devices with their start and end apart: 25 -> 25, of which waited for: 10 -> 11; matrix products, arithmetic and copies ran while one was open for 0% -> 0% of each run, Pallas kernels for 16% -> 16%
where the time goes in v1:
time: 83.6 us; the launch traced here: 83.4 us
  waiting for transfers between devices  47.5 us (57%)
  starting transfers between devices  18.2 us (22%)
  Pallas kernels  14.4 us (17%)
  local copies, waits for them, and re-layouts  3.24 us (4%)
    ppermute x5, waiting for transfers between devices, along_chips(): lax.ppermute(value, 'out', [(r, (r + PAIR) % out_count) for r in range(ou...  27 us
    ppermute x6, waiting for transfers between devices, along_columns(): lax.ppermute(value, 'in', [(s, (s + PAIR * shift) % in_count) for s in ra...  16.9 us
    pallas_call x11, Pallas kernels, kernel_call(): pl.pallas_call(kernel, name=name, out_shape=outputs, in_specs=[pl.BlockSp...  14.4 us
    ppermute x5, starting transfers between devices, along_chips(): lax.ppermute(value, 'out', [(r, (r + PAIR) % out_count) for r in range(ou...  6.74 us
    ppermute x4, starting transfers between devices, across_sides(): return lax.ppermute(value, 'in', [(s, s ^ 1) for s in range(in_count)])  6.2 us
    ppermute x4, waiting for transfers between devices, across_sides(): return lax.ppermute(value, 'in', [(s, s ^ 1) for s in range(in_count)])  3.59 us
    ppermute x6, starting transfers between devices, along_columns(): lax.ppermute(value, 'in', [(s, (s + PAIR * shift) % in_count) for s in ra...  3.46 us
    unnamed x6, local copies, waits for them, and re-layouts  3.24 us
  transfers between devices with their start and end apart: 25, of which 11 were waited for; matrix products, arithmetic and copies ran while one was open for 0% of the time, Pallas kernels for 16%

profile of v1, /device:TPU:0, one launch (start us, length us, event | category | flops | bytes accessed | tf_op | source)
XLA Modules:
  0.0 83.4 jit_solution(16959889757317952738)
XLA Ops:
  0.0 2.9 %collective-permute-start = (bf16[1024,256]{1,0:T(8,128)(2,1)}, bf16[1024,256]{1,0:T(8,128)(2,1)S(1)}, u32[]{:S(2)}, u32[]{:S(2)}) collective-permute-start(bf16[1024,256]{1,0:T(8,128)(2,1)} %refs_1_.1), channel_id=1, source_target_pairs={{0,16},{8,24},{16,0},{24,8},{1,17},{9,25},{17,1},{25,9},{2,18},{10... | collective-permute-start | bytes 1572872 | tf_op jit(solution)/shard_map/ppermute | solution.py:274
  2.9 1.6 %collective-permute-start.5 = (bf16[2,1024,128]{2,1,0:T(8,128)(2,1)}, bf16[2,1024,128]{2,1,0:T(8,128)(2,1)S(1)}, u32[]{:S(2)}, u32[]{:S(2)}) collective-permute-start(bf16[2,1024,128]{2,1,0:T(8,128)(2,1)} %refs_2_.1), channel_id=1, source_target_pairs={{0,2},{1,3},{2,4},{3,5},{4,6},{5,7},{6,0},{7,1},{8,10},{9,11},{10,... | collective-permute-start | bytes 1572872 | tf_op jit(solution)/shard_map/ppermute | solution.py:280
  4.5 2.2 %copy-done = bf16[2,1024,1024]{2,1,0:T(8,128)(2,1)S(1)} copy-done((bf16[2,1024,1024]{2,1,0:T(8,128)(2,1)S(1)}, bf16[2,1024,1024]{2,1,0:T(8,128)(2,1)}, u32[]{:S(2)}) %copy-start) | copy-done | bytes 4194328
  9.1 5.9 %collective-permute-done.refs_1_ = bf16[1024,256]{1,0:T(8,128)(2,1)S(1)} collective-permute-done((bf16[1024,256]{1,0:T(8,128)(2,1)}, bf16[1024,256]{1,0:T(8,128)(2,1)S(1)}, u32[]{:S(2)}, u32[]{:S(2)}) %collective-permute-start) | collective-permute-done | bytes 524320 | tf_op jit(solution)/shard_map/ppermute | solution.py:274
  15.6 2.8 %collective-permute-done.5.refs_0_ = bf16[2,1024,128]{2,1,0:T(8,128)(2,1)S(1)} collective-permute-done((bf16[2,1024,128]{2,1,0:T(8,128)(2,1)}, bf16[2,1024,128]{2,1,0:T(8,128)(2,1)S(1)}, u32[]{:S(2)}, u32[]{:S(2)}) %collective-permute-start.5) | collective-permute-done | bytes 524320 | tf_op jit(solution)/shard_map/ppermute | solution.py:280
  18.9 1.6 %products.7 = (f32[2,1024,128]{2,1,0:T(8,128)S(1)}, s32[1032,128]{1,0:T(8,128)S(1)}) custom-call(bf16[2,1024,1024]{2,1,0:T(8,128)(2,1)S(1)} %get-tuple-element.27.weights, bf16[1024,256]{1,0:T(8,128)(2,1)S(1)} %get-tuple-element.28.refs_0_, bf16[1024,256]{1,0:T(8,128)(2,1)S(1)} %collective-permute-done.refs_1_, ...), custom_call_target="tpu_custom_call" | custom-call | flops 1073741824 | bytes 7868416 | tf_op jit(solution)/shard_map/products/pallas_call | solution.py:83
  20.5 1.6 %collective-permute-start.3 = (s32[1032,128]{1,0:T(8,128)S(1)}, s32[1032,128]{1,0:T(8,128)S(1)}, u32[]{:S(2)}, u32[]{:S(2)}) collective-permute-start(s32[1032,128]{1,0:T(8,128)S(1)} %get-tuple-element.34), channel_id=1, source_target_pairs={{0,1},{1,0},{2,3},{3,2},{4,5},{5,4},{6,7},{7,6},{8,9},{9,8},{10,11... | collective-permute-start | bytes 1585160 | tf_op jit(solution)/shard_map/ppermute | solution.py:277
  22.1 1.5 %products.4 = (f32[2,1024,128]{2,1,0:T(8,128)S(1)}, s32[1032,128]{1,0:T(8,128)S(1)}) custom-call(bf16[2,1024,1024]{2,1,0:T(8,128)(2,1)S(1)} %get-tuple-element.27.weights, bf16[1024,256]{1,0:T(8,128)(2,1)S(1)} %get-tuple-element.28.refs_0_, bf16[1024,256]{1,0:T(8,128)(2,1)S(1)} %collective-permute-done.refs_1_, ...), custom_call_target="tpu_custom_call" | custom-call | flops 1073741824 | bytes 7868416 | tf_op jit(solution)/shard_map/products/pallas_call | solution.py:83
  23.7 1.6 %products.5 = (f32[2,1024,128]{2,1,0:T(8,128)S(1)}, s32[1032,128]{1,0:T(8,128)S(1)}) custom-call(bf16[2,1024,1024]{2,1,0:T(8,128)(2,1)S(1)} %get-tuple-element.27.weights, bf16[1024,256]{1,0:T(8,128)(2,1)S(1)} %get-tuple-element.28.refs_0_, bf16[1024,256]{1,0:T(8,128)(2,1)S(1)} %collective-permute-done.refs_1_, ...), custom_call_target="tpu_custom_call" | custom-call | flops 1073741824 | bytes 7868416 | tf_op jit(solution)/shard_map/products/pallas_call | solution.py:83
  25.3 1.6 %products.6 = (f32[2,1024,128]{2,1,0:T(8,128)S(1)}, s32[1032,128]{1,0:T(8,128)S(1)}) custom-call(bf16[2,1024,1024]{2,1,0:T(8,128)(2,1)S(1)} %get-tuple-element.27.weights, bf16[1024,256]{1,0:T(8,128)(2,1)S(1)} %get-tuple-element.28.refs_0_, bf16[1024,256]{1,0:T(8,128)(2,1)S(1)} %collective-permute-done.refs_1_, ...), custom_call_target="tpu_custom_call" | custom-call | flops 1073741824 | bytes 7868416 | tf_op jit(solution)/shard_map/products/pallas_call | solution.py:83
  26.8 4.1 %collective-permute-done.6.refs_1_ = bf16[2,1024,128]{2,1,0:T(8,128)(2,1)S(1)} collective-permute-done((bf16[2,1024,128]{2,1,0:T(8,128)(2,1)S(1)}, bf16[2,1024,128]{2,1,0:T(8,128)(2,1)S(1)}, u32[]{:S(2)}, u32[]{:S(2)}) %collective-permute-start.6) | collective-permute-done | bytes 524320 | tf_op jit(solution)/shard_map/ppermute | solution.py:274
  30.9 2.3 %collective-permute-done.11.refs_0_ = bf16[2,1024,128]{2,1,0:T(8,128)(2,1)S(1)} collective-permute-done((bf16[2,1024,128]{2,1,0:T(8,128)(2,1)S(1)}, bf16[2,1024,128]{2,1,0:T(8,128)(2,1)S(1)}, u32[]{:S(2)}, u32[]{:S(2)}) %collective-permute-start.11) | collective-permute-done | bytes 524320 | tf_op jit(solution)/shard_map/ppermute | solution.py:280
  34.5 1.5 %collective-permute-start.4 = (s32[1032,128]{1,0:T(8,128)S(1)}, s32[1032,128]{1,0:T(8,128)S(1)}, u32[]{:S(2)}, u32[]{:S(2)}) collective-permute-start(s32[1032,128]{1,0:T(8,128)S(1)} %get-tuple-element.35), channel_id=1, source_target_pairs={{0,1},{1,0},{2,3},{3,2},{4,5},{5,4},{6,7},{7,6},{8,9},{9,8},{10,11... | collective-permute-start | bytes 1585160 | tf_op jit(solution)/shard_map/ppermute | solution.py:277
  36.5 8.3 %collective-permute-done.13.refs_1_ = bf16[2,1024,128]{2,1,0:T(8,128)(2,1)S(1)} collective-permute-done((bf16[2,1024,128]{2,1,0:T(8,128)(2,1)S(1)}, bf16[2,1024,128]{2,1,0:T(8,128)(2,1)S(1)}, u32[]{:S(2)}, u32[]{:S(2)}) %collective-permute-start.13) | collective-permute-done | bytes 524320 | tf_op jit(solution)/shard_map/ppermute | solution.py:274
  44.8 2.5 %collective-permute-done.19.refs_0_ = bf16[2,1024,128]{2,1,0:T(8,128)(2,1)S(1)} collective-permute-done((bf16[2,1024,128]{2,1,0:T(8,128)(2,1)S(1)}, bf16[2,1024,128]{2,1,0:T(8,128)(2,1)S(1)}, u32[]{:S(2)}, u32[]{:S(2)}) %collective-permute-start.19) | collective-permute-done | bytes 524320 | tf_op jit(solution)/shard_map/ppermute | solution.py:280
  48.4 1.5 %partial_sums.3 = s32[520,128]{1,0:T(8,128)S(1)} custom-call(s32[4,8]{1,0:T(4,128)S(1)} %copy-done.2, f32[2,1024,128]{2,1,0:T(8,128)S(1)} %get-tuple-element.36.kept, s32[1032,128]{1,0:T(8,128)S(1)} %collective-permute-done.3.received, bf16[2,1024,128]{2,1,0:T(8,128)(2,1)S(1)} %collective-permute-done.5.refs_0_, ...), custom_call_target="tpu_custom_call" | custom-call | flops 2097152 | bytes 3940480 | tf_op jit(solution)/shard_map/partial_sums/pallas_call | solution.py:83
  50.9 1.5 %collective-permute-start.9 = (s32[1032,128]{1,0:T(8,128)S(1)}, s32[1032,128]{1,0:T(8,128)S(1)}, u32[]{:S(2)}, u32[]{:S(2)}) collective-permute-start(s32[1032,128]{1,0:T(8,128)S(1)} %get-tuple-element.38), channel_id=1, source_target_pairs={{0,1},{1,0},{2,3},{3,2},{4,5},{5,4},{6,7},{7,6},{8,9},{9,8},{10,11... | collective-permute-start | bytes 1585160 | tf_op jit(solution)/shard_map/ppermute | solution.py:277
  52.4 5.1 %collective-permute-done.20.refs_1_ = bf16[2,1024,128]{2,1,0:T(8,128)(2,1)S(1)} collective-permute-done((bf16[2,1024,128]{2,1,0:T(8,128)(2,1)S(1)}, bf16[2,1024,128]{2,1,0:T(8,128)(2,1)S(1)}, u32[]{:S(2)}, u32[]{:S(2)}) %collective-permute-start.20) | collective-permute-done | bytes 524320 | tf_op jit(solution)/shard_map/ppermute | solution.py:274
  59.9 1.5 %partial_sums.4 = s32[520,128]{1,0:T(8,128)S(1)} custom-call(s32[4,8]{1,0:T(4,128)S(1)} %copy-done.2, f32[2,1024,128]{2,1,0:T(8,128)S(1)} %get-tuple-element.40.kept, s32[1032,128]{1,0:T(8,128)S(1)} %collective-permute-done.4.received, bf16[2,1024,128]{2,1,0:T(8,128)(2,1)S(1)} %collective-permute-done.11.refs_0_, ...), custom_call_target="tpu_custom_call" | custom-call | flops 2097152 | bytes 3940480 | tf_op jit(solution)/shard_map/partial_sums/pallas_call | solution.py:83
  61.5 3.6 %collective-permute-done.9.received = s32[1032,128]{1,0:T(8,128)S(1)} collective-permute-done((s32[1032,128]{1,0:T(8,128)S(1)}, s32[1032,128]{1,0:T(8,128)S(1)}, u32[]{:S(2)}, u32[]{:S(2)}) %collective-permute-start.9) | collective-permute-done | bytes 528416 | tf_op jit(solution)/shard_map/ppermute | solution.py:277
  65.1 1.5 %collective-permute-start.16 = (s32[1032,128]{1,0:T(8,128)S(1)}, s32[1032,128]{1,0:T(8,128)S(1)}, u32[]{:S(2)}, u32[]{:S(2)}) collective-permute-start(s32[1032,128]{1,0:T(8,128)S(1)} %get-tuple-element.43), channel_id=1, source_target_pairs={{0,1},{1,0},{2,3},{3,2},{4,5},{5,4},{6,7},{7,6},{8,9},{9,8},{10,11... | collective-permute-start | bytes 1585160 | tf_op jit(solution)/shard_map/ppermute | solution.py:277
  66.6 1.5 %partial_sums.5 = s32[520,128]{1,0:T(8,128)S(1)} custom-call(s32[4,8]{1,0:T(4,128)S(1)} %copy-done.2, f32[2,1024,128]{2,1,0:T(8,128)S(1)} %get-tuple-element.46.kept, s32[1032,128]{1,0:T(8,128)S(1)} %collective-permute-done.9.received, bf16[2,1024,128]{2,1,0:T(8,128)(2,1)S(1)} %collective-permute-done.19.refs_0_, ...), custom_call_target="tpu_custom_call" | custom-call | flops 2097152 | bytes 3940480 | tf_op jit(solution)/shard_map/partial_sums/pallas_call | solution.py:83
  69.2 3.5 %collective-permute-done.18.refs_1_ = bf16[2,1024,128]{2,1,0:T(8,128)(2,1)S(1)} collective-permute-done((bf16[2,1024,128]{2,1,0:T(8,128)(2,1)}, bf16[2,1024,128]{2,1,0:T(8,128)(2,1)S(1)}, u32[]{:S(2)}, u32[]{:S(2)}) %collective-permute-start.18) | collective-permute-done | bytes 524320 | tf_op jit(solution)/shard_map/ppermute | solution.py:274
  72.7 8.4 %collective-permute-done.17.refs_1_ = s32[520,128]{1,0:T(8,128)S(1)} collective-permute-done((s32[520,128]{1,0:T(8,128)S(1)}, s32[520,128]{1,0:T(8,128)S(1)}, u32[]{:S(2)}, u32[]{:S(2)}) %collective-permute-start.17) | collective-permute-done | bytes 266272 | tf_op jit(solution)/shard_map/ppermute | solution.py:280
  (43 shorter events, 13.2 us)
Async XLA Ops:
  0.0 15.1 %collective-permute-start = (bf16[1024,256]{1,0:T(8,128)(2,1)}, bf16[1024,256]{1,0:T(8,128)(2,1)S(1)}, u32[]{:S(2)}, u32[]{:S(2)}) collective-permute-start(bf16[1024,256]{1,0:T(8,128)(2,1)} %refs_1_.1), channel_id=1, source_target_pairs={{0,16},{8,24},{16,0},{24,8},{1,17},{9,25},{17,1},{25,9},{2,18},{10... | collective-permute-start | bytes 1572872 | tf_op jit(solution)/shard_map/ppermute | solution.py:274
  2.9 15.5 %collective-permute-start.5 = (bf16[2,1024,128]{2,1,0:T(8,128)(2,1)}, bf16[2,1024,128]{2,1,0:T(8,128)(2,1)S(1)}, u32[]{:S(2)}, u32[]{:S(2)}) collective-permute-start(bf16[2,1024,128]{2,1,0:T(8,128)(2,1)} %refs_2_.1), channel_id=1, source_target_pairs={{0,2},{1,3},{2,4},{3,5},{4,6},{5,7},{6,0},{7,1},{8,10},{9,11},{10,... | collective-permute-start | bytes 1572872 | tf_op jit(solution)/shard_map/ppermute | solution.py:280
  4.5 14.4 %collective-permute-start.1 = (bf16[1024,256]{1,0:T(8,128)(2,1)}, bf16[1024,256]{1,0:T(8,128)(2,1)S(1)}, u32[]{:S(2)}, u32[]{:S(2)}) collective-permute-start(bf16[1024,256]{1,0:T(8,128)(2,1)} %refs_1_.1), channel_id=1, source_target_pairs={{0,8},{8,0},{16,24},{24,16},{1,9},{9,1},{17,25},{25,17},{2,10},{10... | collective-permute-start | bytes 1572872 | tf_op jit(solution)/shard_map/ppermute | solution.py:271
  15.1 11.8 %collective-permute-start.12 = (bf16[2,1024,128]{2,1,0:T(8,128)(2,1)}, bf16[2,1024,128]{2,1,0:T(8,128)(2,1)S(1)}, u32[]{:S(2)}, u32[]{:S(2)}) collective-permute-start(bf16[2,1024,128]{2,1,0:T(8,128)(2,1)} %refs_2_.1), channel_id=1, source_target_pairs={{0,8},{8,0},{16,24},{24,16},{1,9},{9,1},{17,25},{25,17},{2,10},{10... | collective-permute-start | bytes 1572872 | tf_op jit(solution)/shard_map/ppermute | solution.py:271
  18.4 12.5 %collective-permute-start.6 = (bf16[2,1024,128]{2,1,0:T(8,128)(2,1)S(1)}, bf16[2,1024,128]{2,1,0:T(8,128)(2,1)S(1)}, u32[]{:S(2)}, u32[]{:S(2)}) collective-permute-start(bf16[2,1024,128]{2,1,0:T(8,128)(2,1)S(1)} %collective-permute-done.5.refs_0_), channel_id=1, source_target_pairs={{0,16},{8,24},{16,0},{24,8},{1,17},{9,25},{17,1},{25,9},{2,18},{10... | collective-permute-start | bytes 1572872 | tf_op jit(solution)/shard_map/ppermute | solution.py:274
  18.9 14.3 %collective-permute-start.11 = (bf16[2,1024,128]{2,1,0:T(8,128)(2,1)S(1)}, bf16[2,1024,128]{2,1,0:T(8,128)(2,1)S(1)}, u32[]{:S(2)}, u32[]{:S(2)}) collective-permute-start(bf16[2,1024,128]{2,1,0:T(8,128)(2,1)S(1)} %collective-permute-done.5.refs_0_), channel_id=1, source_target_pairs={{0,2},{1,3},{2,4},{3,5},{4,6},{5,7},{6,0},{7,1},{8,10},{9,11},{10,... | collective-permute-start | bytes 1572872 | tf_op jit(solution)/shard_map/ppermute | solution.py:280
  20.5 14.0 %collective-permute-start.3 = (s32[1032,128]{1,0:T(8,128)S(1)}, s32[1032,128]{1,0:T(8,128)S(1)}, u32[]{:S(2)}, u32[]{:S(2)}) collective-permute-start(s32[1032,128]{1,0:T(8,128)S(1)} %get-tuple-element.34), channel_id=1, source_target_pairs={{0,1},{1,0},{2,3},{3,2},{4,5},{5,4},{6,7},{7,6},{8,9},{9,8},{10,11... | collective-permute-start | bytes 1585160 | tf_op jit(solution)/shard_map/ppermute | solution.py:277
  33.2 11.6 %collective-permute-start.13 = (bf16[2,1024,128]{2,1,0:T(8,128)(2,1)S(1)}, bf16[2,1024,128]{2,1,0:T(8,128)(2,1)S(1)}, u32[]{:S(2)}, u32[]{:S(2)}) collective-permute-start(bf16[2,1024,128]{2,1,0:T(8,128)(2,1)S(1)} %collective-permute-done.11.refs_0_), channel_id=1, source_target_pairs={{0,16},{8,24},{16,0},{24,8},{1,17},{9,25},{17,1},{25,9},{2,18},{10... | collective-permute-start | bytes 1572872 | tf_op jit(solution)/shard_map/ppermute | solution.py:274
  34.5 12.9 %collective-permute-start.19 = (bf16[2,1024,128]{2,1,0:T(8,128)(2,1)S(1)}, bf16[2,1024,128]{2,1,0:T(8,128)(2,1)S(1)}, u32[]{:S(2)}, u32[]{:S(2)}) collective-permute-start(bf16[2,1024,128]{2,1,0:T(8,128)(2,1)S(1)} %collective-permute-done.11.refs_0_), channel_id=1, source_target_pairs={{0,2},{1,3},{2,4},{3,5},{4,6},{5,7},{6,0},{7,1},{8,10},{9,11},{10,... | collective-permute-start | bytes 1572872 | tf_op jit(solution)/shard_map/ppermute | solution.py:280
  34.5 16.2 %collective-permute-start.4 = (s32[1032,128]{1,0:T(8,128)S(1)}, s32[1032,128]{1,0:T(8,128)S(1)}, u32[]{:S(2)}, u32[]{:S(2)}) collective-permute-start(s32[1032,128]{1,0:T(8,128)S(1)} %get-tuple-element.35), channel_id=1, source_target_pairs={{0,1},{1,0},{2,3},{3,2},{4,5},{5,4},{6,7},{7,6},{8,9},{9,8},{10,11... | collective-permute-start | bytes 1585160 | tf_op jit(solution)/shard_map/ppermute | solution.py:277
  36.0 12.4 %collective-permute-start.7 = (bf16[2,1024,128]{2,1,0:T(8,128)(2,1)S(1)}, bf16[2,1024,128]{2,1,0:T(8,128)(2,1)S(1)}, u32[]{:S(2)}, u32[]{:S(2)}) collective-permute-start(bf16[2,1024,128]{2,1,0:T(8,128)(2,1)S(1)} %collective-permute-done.5.refs_0_), channel_id=1, source_target_pairs={{0,8},{8,0},{16,24},{24,16},{1,9},{9,1},{17,25},{25,17},{2,10},{10... | collective-permute-start | bytes 1572872 | tf_op jit(solution)/shard_map/ppermute | solution.py:271
  36.0 12.4 %collective-permute-start.8 = (bf16[2,1024,128]{2,1,0:T(8,128)(2,1)S(1)}, bf16[2,1024,128]{2,1,0:T(8,128)(2,1)S(1)}, u32[]{:S(2)}, u32[]{:S(2)}) collective-permute-start(bf16[2,1024,128]{2,1,0:T(8,128)(2,1)S(1)} %collective-permute-done.6.refs_1_), channel_id=1, source_target_pairs={{0,8},{8,0},{16,24},{24,16},{1,9},{9,1},{17,25},{25,17},{2,10},{10... | collective-permute-start | bytes 1572872 | tf_op jit(solution)/shard_map/ppermute | solution.py:271
  47.3 10.1 %collective-permute-start.20 = (bf16[2,1024,128]{2,1,0:T(8,128)(2,1)S(1)}, bf16[2,1024,128]{2,1,0:T(8,128)(2,1)S(1)}, u32[]{:S(2)}, u32[]{:S(2)}) collective-permute-start(bf16[2,1024,128]{2,1,0:T(8,128)(2,1)S(1)} %collective-permute-done.19.refs_0_), channel_id=1, source_target_pairs={{0,16},{8,24},{16,0},{24,8},{1,17},{9,25},{17,1},{25,9},{2,18},{10... | collective-permute-start | bytes 1572872 | tf_op jit(solution)/shard_map/ppermute | solution.py:274
  48.4 9.1 %collective-permute-start.14 = (bf16[2,1024,128]{2,1,0:T(8,128)(2,1)S(1)}, bf16[2,1024,128]{2,1,0:T(8,128)(2,1)S(1)}, u32[]{:S(2)}, u32[]{:S(2)}) collective-permute-start(bf16[2,1024,128]{2,1,0:T(8,128)(2,1)S(1)} %collective-permute-done.11.refs_0_), channel_id=1, source_target_pairs={{0,8},{8,0},{16,24},{24,16},{1,9},{9,1},{17,25},{25,17},{2,10},{10... | collective-permute-start | bytes 1572872 | tf_op jit(solution)/shard_map/ppermute | solution.py:271
  49.9 9.0 %collective-permute-start.10 = (s32[520,128]{1,0:T(8,128)S(1)}, s32[520,128]{1,0:T(8,128)S(1)}, u32[]{:S(2)}, u32[]{:S(2)}) collective-permute-start(s32[520,128]{1,0:T(8,128)S(1)} %partial_sums.3), channel_id=1, source_target_pairs={{0,6},{1,7},{2,0},{3,1},{4,2},{5,3},{6,4},{7,5},{8,14},{9,15},{10,... | collective-permute-start | bytes 798728 | tf_op jit(solution)/shard_map/ppermute | solution.py:280
  50.6 9.3 %collective-permute-start.15 = (bf16[2,1024,128]{2,1,0:T(8,128)(2,1)S(1)}, bf16[2,1024,128]{2,1,0:T(8,128)(2,1)S(1)}, u32[]{:S(2)}, u32[]{:S(2)}) collective-permute-start(bf16[2,1024,128]{2,1,0:T(8,128)(2,1)S(1)} %collective-permute-done.13.refs_1_), channel_id=1, source_target_pairs={{0,8},{8,0},{16,24},{24,16},{1,9},{9,1},{17,25},{25,17},{2,10},{10... | collective-permute-start | bytes 1572872 | tf_op jit(solution)/shard_map/ppermute | solution.py:271
  50.9 14.2 %collective-permute-start.9 = (s32[1032,128]{1,0:T(8,128)S(1)}, s32[1032,128]{1,0:T(8,128)S(1)}, u32[]{:S(2)}, u32[]{:S(2)}) collective-permute-start(s32[1032,128]{1,0:T(8,128)S(1)} %get-tuple-element.38), channel_id=1, source_target_pairs={{0,1},{1,0},{2,3},{3,2},{4,5},{5,4},{6,7},{7,6},{8,9},{9,8},{10,11... | collective-permute-start | bytes 1585160 | tf_op jit(solution)/shard_map/ppermute | solution.py:277
  57.5 9.1 %collective-permute-start.21 = (bf16[2,1024,128]{2,1,0:T(8,128)(2,1)S(1)}, bf16[2,1024,128]{2,1,0:T(8,128)(2,1)S(1)}, u32[]{:S(2)}, u32[]{:S(2)}) collective-permute-start(bf16[2,1024,128]{2,1,0:T(8,128)(2,1)S(1)} %collective-permute-done.19.refs_0_), channel_id=1, source_target_pairs={{0,8},{8,0},{16,24},{24,16},{1,9},{9,1},{17,25},{25,17},{2,10},{10... | collective-permute-start | bytes 1572872 | tf_op jit(solution)/shard_map/ppermute | solution.py:271
  57.5 9.1 %collective-permute-start.22 = (bf16[2,1024,128]{2,1,0:T(8,128)(2,1)S(1)}, bf16[2,1024,128]{2,1,0:T(8,128)(2,1)S(1)}, u32[]{:S(2)}, u32[]{:S(2)}) collective-permute-start(bf16[2,1024,128]{2,1,0:T(8,128)(2,1)S(1)} %collective-permute-done.20.refs_1_), channel_id=1, source_target_pairs={{0,8},{8,0},{16,24},{24,16},{1,9},{9,1},{17,25},{25,17},{2,10},{10... | collective-permute-start | bytes 1572872 | tf_op jit(solution)/shard_map/ppermute | solution.py:271
  58.9 13.8 %collective-permute-start.18 = (bf16[2,1024,128]{2,1,0:T(8,128)(2,1)}, bf16[2,1024,128]{2,1,0:T(8,128)(2,1)S(1)}, u32[]{:S(2)}, u32[]{:S(2)}) collective-permute-start(bf16[2,1024,128]{2,1,0:T(8,128)(2,1)} %refs_2_.1), channel_id=1, source_target_pairs={{0,16},{8,24},{16,0},{24,8},{1,17},{9,25},{17,1},{25,9},{2,18},{10... | collective-permute-start | bytes 1572872 | tf_op jit(solution)/shard_map/ppermute | solution.py:274
  61.4 19.6 %collective-permute-start.17 = (s32[520,128]{1,0:T(8,128)S(1)}, s32[520,128]{1,0:T(8,128)S(1)}, u32[]{:S(2)}, u32[]{:S(2)}) collective-permute-start(s32[520,128]{1,0:T(8,128)S(1)} %partial_sums.4), channel_id=1, source_target_pairs={{0,4},{1,5},{2,6},{3,7},{4,0},{5,1},{6,2},{7,3},{8,12},{9,13},{10,... | collective-permute-start | bytes 798728 | tf_op jit(solution)/shard_map/ppermute | solution.py:280
  65.1 16.2 %collective-permute-start.16 = (s32[1032,128]{1,0:T(8,128)S(1)}, s32[1032,128]{1,0:T(8,128)S(1)}, u32[]{:S(2)}, u32[]{:S(2)}) collective-permute-start(s32[1032,128]{1,0:T(8,128)S(1)} %get-tuple-element.43), channel_id=1, source_target_pairs={{0,1},{1,0},{2,3},{3,2},{4,5},{5,4},{6,7},{7,6},{8,9},{9,8},{10,11... | collective-permute-start | bytes 1585160 | tf_op jit(solution)/shard_map/ppermute | solution.py:277
  68.1 14.5 %collective-permute-start.24 = (s32[520,128]{1,0:T(8,128)S(1)}, s32[520,128]{1,0:T(8,128)S(1)}, u32[]{:S(2)}, u32[]{:S(2)}) collective-permute-start(s32[520,128]{1,0:T(8,128)S(1)} %partial_sums.5), channel_id=1, source_target_pairs={{0,2},{1,3},{2,4},{3,5},{4,6},{5,7},{6,0},{7,1},{8,10},{9,11},{10,... | collective-permute-start | bytes 798728 | tf_op jit(solution)/shard_map/ppermute | solution.py:280
  72.7 8.6 %collective-permute-start.23 = (bf16[2,1024,128]{2,1,0:T(8,128)(2,1)S(1)}, bf16[2,1024,128]{2,1,0:T(8,128)(2,1)S(1)}, u32[]{:S(2)}, u32[]{:S(2)}) collective-permute-start(bf16[2,1024,128]{2,1,0:T(8,128)(2,1)S(1)} %collective-permute-done.18.refs_1_), channel_id=1, source_target_pairs={{0,8},{8,0},{16,24},{24,16},{1,9},{9,1},{17,25},{25,17},{2,10},{10... | collective-permute-start | bytes 1572872 | tf_op jit(solution)/shard_map/ppermute | solution.py:271
  (4 other events, 30.2 us)

commit v2 on v1

--- a/solution.py
+++ b/solution.py
@@ -297,15 +297,17 @@
         earlier = [[far_field], [*sent.values(), core_own, far[-1]]][place] if place < 2 else far[-1:]
         far.append(along_chips(after(rings[step], *earlier)))
 
-    received, coming = {}, []
+    received, coming, partials = {}, [], []
 
     def send_sums(place):
         step = order[place]
         swapped = [received[step]] if place == 1 else []
-        pieces[step] = [near(rings[step]), near(far[place + 1]), near(across_cores(rings[step]))]
+        made = partials if place == 1 else []
+        pieces[step] = [near(rings[step]), near(far[place + 1]), near(across_cores(after(rings[step], *made)))]
         pieces[step].append(near(across_cores(after(far[place + 1], *swapped))))
         ready = after(kept[step], *(coming[-1:] if place < columns - 2 else []))
         partial = partial_sums(block_table, ready, received[step], pieces[step])
+        partials.append(partial)
         coming.append(near(along_columns(partial, -step)))
         return partial
 

time: 83.6 us -> 84.2 us (level)
  waiting for transfers between devices: 47.5 us -> 48.6 us
where the time goes in v2:
time: 84.2 us; the launch traced here: 83.9 us
  waiting for transfers between devices  48.6 us (58%)
  starting transfers between devices  17.6 us (21%)
  Pallas kernels  14.4 us (17%)
  local copies, waits for them, and re-layouts  3.24 us (4%)
    ppermute x5, waiting for transfers between devices, along_chips(): lax.ppermute(value, 'out', [(r, (r + PAIR) % out_count) for r in range(ou...  27.7 us
    ppermute x6, waiting for transfers between devices, along_columns(): lax.ppermute(value, 'in', [(s, (s + PAIR * shift) % in_count) for s in ra...  17.2 us
    pallas_call x11, Pallas kernels, kernel_call(): pl.pallas_call(kernel, name=name, out_shape=outputs, in_specs=[pl.BlockSp...  14.4 us
    ppermute x5, starting transfers between devices, along_chips(): lax.ppermute(value, 'out', [(r, (r + PAIR) % out_count) for r in range(ou...  6.74 us
    ppermute x4, starting transfers between devices, across_sides(): return lax.ppermute(value, 'in', [(s, s ^ 1) for s in range(in_count)])  6.2 us
    ppermute x4, waiting for transfers between devices, across_sides(): return lax.ppermute(value, 'in', [(s, s ^ 1) for s in range(in_count)])  3.73 us
    ppermute x6, starting transfers between devices, along_columns(): lax.ppermute(value, 'in', [(s, (s + PAIR * shift) % in_count) for s in ra...  3.56 us
    unnamed x6, local copies, waits for them, and re-layouts  3.24 us
  transfers between devices with their start and end apart: 25, of which 11 were waited for; matrix products, arithmetic and copies ran while one was open for 0% of the time, Pallas kernels for 16%

profile of v2, /device:TPU:0, one launch (start us, length us, event | category | flops | bytes accessed | tf_op | source)
XLA Modules:
  0.0 83.9 jit_solution(4426898163585946820)
XLA Ops:
  0.0 2.9 %collective-permute-start = (bf16[1024,256]{1,0:T(8,128)(2,1)}, bf16[1024,256]{1,0:T(8,128)(2,1)S(1)}, u32[]{:S(2)}, u32[]{:S(2)}) collective-permute-start(bf16[1024,256]{1,0:T(8,128)(2,1)} %refs_1_.1), channel_id=1, source_target_pairs={{0,16},{8,24},{16,0},{24,8},{1,17},{9,25},{17,1},{25,9},{2,18},{10... | collective-permute-start | bytes 1572872 | tf_op jit(solution)/shard_map/ppermute | solution.py:274
  2.9 1.6 %collective-permute-start.5 = (bf16[2,1024,128]{2,1,0:T(8,128)(2,1)}, bf16[2,1024,128]{2,1,0:T(8,128)(2,1)S(1)}, u32[]{:S(2)}, u32[]{:S(2)}) collective-permute-start(bf16[2,1024,128]{2,1,0:T(8,128)(2,1)} %refs_2_.1), channel_id=1, source_target_pairs={{0,2},{1,3},{2,4},{3,5},{4,6},{5,7},{6,0},{7,1},{8,10},{9,11},{10,... | collective-permute-start | bytes 1572872 | tf_op jit(solution)/shard_map/ppermute | solution.py:280
  4.5 2.2 %copy-done = bf16[2,1024,1024]{2,1,0:T(8,128)(2,1)S(1)} copy-done((bf16[2,1024,1024]{2,1,0:T(8,128)(2,1)S(1)}, bf16[2,1024,1024]{2,1,0:T(8,128)(2,1)}, u32[]{:S(2)}) %copy-start) | copy-done | bytes 4194328
  9.1 5.9 %collective-permute-done.refs_1_ = bf16[1024,256]{1,0:T(8,128)(2,1)S(1)} collective-permute-done((bf16[1024,256]{1,0:T(8,128)(2,1)}, bf16[1024,256]{1,0:T(8,128)(2,1)S(1)}, u32[]{:S(2)}, u32[]{:S(2)}) %collective-permute-start) | collective-permute-done | bytes 524320 | tf_op jit(solution)/shard_map/ppermute | solution.py:274
  15.6 2.8 %collective-permute-done.5.refs_0_ = bf16[2,1024,128]{2,1,0:T(8,128)(2,1)S(1)} collective-permute-done((bf16[2,1024,128]{2,1,0:T(8,128)(2,1)}, bf16[2,1024,128]{2,1,0:T(8,128)(2,1)S(1)}, u32[]{:S(2)}, u32[]{:S(2)}) %collective-permute-start.5) | collective-permute-done | bytes 524320 | tf_op jit(solution)/shard_map/ppermute | solution.py:280
  18.9 1.6 %products.7 = (f32[2,1024,128]{2,1,0:T(8,128)S(1)}, s32[1032,128]{1,0:T(8,128)S(1)}) custom-call(bf16[2,1024,1024]{2,1,0:T(8,128)(2,1)S(1)} %get-tuple-element.28.weights, bf16[1024,256]{1,0:T(8,128)(2,1)S(1)} %get-tuple-element.29.refs_0_, bf16[1024,256]{1,0:T(8,128)(2,1)S(1)} %collective-permute-done.refs_1_, ...), custom_call_target="tpu_custom_call" | custom-call | flops 1073741824 | bytes 7868416 | tf_op jit(solution)/shard_map/products/pallas_call | solution.py:83
  20.5 1.6 %collective-permute-start.3 = (s32[1032,128]{1,0:T(8,128)S(1)}, s32[1032,128]{1,0:T(8,128)S(1)}, u32[]{:S(2)}, u32[]{:S(2)}) collective-permute-start(s32[1032,128]{1,0:T(8,128)S(1)} %get-tuple-element.35), channel_id=1, source_target_pairs={{0,1},{1,0},{2,3},{3,2},{4,5},{5,4},{6,7},{7,6},{8,9},{9,8},{10,11... | collective-permute-start | bytes 1585160 | tf_op jit(solution)/shard_map/ppermute | solution.py:277
  22.1 1.5 %products.4 = (f32[2,1024,128]{2,1,0:T(8,128)S(1)}, s32[1032,128]{1,0:T(8,128)S(1)}) custom-call(bf16[2,1024,1024]{2,1,0:T(8,128)(2,1)S(1)} %get-tuple-element.28.weights, bf16[1024,256]{1,0:T(8,128)(2,1)S(1)} %get-tuple-element.29.refs_0_, bf16[1024,256]{1,0:T(8,128)(2,1)S(1)} %collective-permute-done.refs_1_, ...), custom_call_target="tpu_custom_call" | custom-call | flops 1073741824 | bytes 7868416 | tf_op jit(solution)/shard_map/products/pallas_call | solution.py:83
  23.7 1.6 %products.5 = (f32[2,1024,128]{2,1,0:T(8,128)S(1)}, s32[1032,128]{1,0:T(8,128)S(1)}) custom-call(bf16[2,1024,1024]{2,1,0:T(8,128)(2,1)S(1)} %get-tuple-element.28.weights, bf16[1024,256]{1,0:T(8,128)(2,1)S(1)} %get-tuple-element.29.refs_0_, bf16[1024,256]{1,0:T(8,128)(2,1)S(1)} %collective-permute-done.refs_1_, ...), custom_call_target="tpu_custom_call" | custom-call | flops 1073741824 | bytes 7868416 | tf_op jit(solution)/shard_map/products/pallas_call | solution.py:83
  25.3 1.6 %products.6 = (f32[2,1024,128]{2,1,0:T(8,128)S(1)}, s32[1032,128]{1,0:T(8,128)S(1)}) custom-call(bf16[2,1024,1024]{2,1,0:T(8,128)(2,1)S(1)} %get-tuple-element.28.weights, bf16[1024,256]{1,0:T(8,128)(2,1)S(1)} %get-tuple-element.29.refs_0_, bf16[1024,256]{1,0:T(8,128)(2,1)S(1)} %collective-permute-done.refs_1_, ...), custom_call_target="tpu_custom_call" | custom-call | flops 1073741824 | bytes 7868416 | tf_op jit(solution)/shard_map/products/pallas_call | solution.py:83
  26.8 4.1 %collective-permute-done.6.refs_1_ = bf16[2,1024,128]{2,1,0:T(8,128)(2,1)S(1)} collective-permute-done((bf16[2,1024,128]{2,1,0:T(8,128)(2,1)S(1)}, bf16[2,1024,128]{2,1,0:T(8,128)(2,1)S(1)}, u32[]{:S(2)}, u32[]{:S(2)}) %collective-permute-start.6) | collective-permute-done | bytes 524320 | tf_op jit(solution)/shard_map/ppermute | solution.py:274
  30.9 2.3 %collective-permute-done.11.refs_0_ = bf16[2,1024,128]{2,1,0:T(8,128)(2,1)S(1)} collective-permute-done((bf16[2,1024,128]{2,1,0:T(8,128)(2,1)S(1)}, bf16[2,1024,128]{2,1,0:T(8,128)(2,1)S(1)}, u32[]{:S(2)}, u32[]{:S(2)}) %collective-permute-start.11) | collective-permute-done | bytes 524320 | tf_op jit(solution)/shard_map/ppermute | solution.py:280
  35.0 1.5 %collective-permute-start.4 = (s32[1032,128]{1,0:T(8,128)S(1)}, s32[1032,128]{1,0:T(8,128)S(1)}, u32[]{:S(2)}, u32[]{:S(2)}) collective-permute-start(s32[1032,128]{1,0:T(8,128)S(1)} %get-tuple-element.36), channel_id=1, source_target_pairs={{0,1},{1,0},{2,3},{3,2},{4,5},{5,4},{6,7},{7,6},{8,9},{9,8},{10,11... | collective-permute-start | bytes 1585160 | tf_op jit(solution)/shard_map/ppermute | solution.py:277
  36.5 8.3 %collective-permute-done.13.refs_1_ = bf16[2,1024,128]{2,1,0:T(8,128)(2,1)S(1)} collective-permute-done((bf16[2,1024,128]{2,1,0:T(8,128)(2,1)S(1)}, bf16[2,1024,128]{2,1,0:T(8,128)(2,1)S(1)}, u32[]{:S(2)}, u32[]{:S(2)}) %collective-permute-start.13) | collective-permute-done | bytes 524320 | tf_op jit(solution)/shard_map/ppermute | solution.py:274
  44.8 2.5 %collective-permute-done.19.refs_0_ = bf16[2,1024,128]{2,1,0:T(8,128)(2,1)S(1)} collective-permute-done((bf16[2,1024,128]{2,1,0:T(8,128)(2,1)S(1)}, bf16[2,1024,128]{2,1,0:T(8,128)(2,1)S(1)}, u32[]{:S(2)}, u32[]{:S(2)}) %collective-permute-start.19) | collective-permute-done | bytes 524320 | tf_op jit(solution)/shard_map/ppermute | solution.py:280
  48.4 1.5 %partial_sums.3 = s32[520,128]{1,0:T(8,128)S(1)} custom-call(s32[4,8]{1,0:T(4,128)S(1)} %copy-done.2, f32[2,1024,128]{2,1,0:T(8,128)S(1)} %get-tuple-element.37.kept, s32[1032,128]{1,0:T(8,128)S(1)} %collective-permute-done.3.received, bf16[2,1024,128]{2,1,0:T(8,128)(2,1)S(1)} %collective-permute-done.5.refs_0_, ...), custom_call_target="tpu_custom_call" | custom-call | flops 2097152 | bytes 3940480 | tf_op jit(solution)/shard_map/partial_sums/pallas_call | solution.py:83
  50.7 1.5 %collective-permute-start.9 = (s32[1032,128]{1,0:T(8,128)S(1)}, s32[1032,128]{1,0:T(8,128)S(1)}, u32[]{:S(2)}, u32[]{:S(2)}) collective-permute-start(s32[1032,128]{1,0:T(8,128)S(1)} %get-tuple-element.39), channel_id=1, source_target_pairs={{0,1},{1,0},{2,3},{3,2},{4,5},{5,4},{6,7},{7,6},{8,9},{9,8},{10,11... | collective-permute-start | bytes 1585160 | tf_op jit(solution)/shard_map/ppermute | solution.py:277
  52.2 5.2 %collective-permute-done.20.refs_1_ = bf16[2,1024,128]{2,1,0:T(8,128)(2,1)S(1)} collective-permute-done((bf16[2,1024,128]{2,1,0:T(8,128)(2,1)S(1)}, bf16[2,1024,128]{2,1,0:T(8,128)(2,1)S(1)}, u32[]{:S(2)}, u32[]{:S(2)}) %collective-permute-start.20) | collective-permute-done | bytes 524320 | tf_op jit(solution)/shard_map/ppermute | solution.py:274
  59.8 1.5 %partial_sums.4 = s32[520,128]{1,0:T(8,128)S(1)} custom-call(s32[4,8]{1,0:T(4,128)S(1)} %copy-done.2, f32[2,1024,128]{2,1,0:T(8,128)S(1)} %get-tuple-element.41.kept, s32[1032,128]{1,0:T(8,128)S(1)} %collective-permute-done.4.received, bf16[2,1024,128]{2,1,0:T(8,128)(2,1)S(1)} %collective-permute-done.11.refs_0_, ...), custom_call_target="tpu_custom_call" | custom-call | flops 2097152 | bytes 3940480 | tf_op jit(solution)/shard_map/partial_sums/pallas_call | solution.py:83
  61.4 3.7 %collective-permute-done.9.received = s32[1032,128]{1,0:T(8,128)S(1)} collective-permute-done((s32[1032,128]{1,0:T(8,128)S(1)}, s32[1032,128]{1,0:T(8,128)S(1)}, u32[]{:S(2)}, u32[]{:S(2)}) %collective-permute-start.9) | collective-permute-done | bytes 528416 | tf_op jit(solution)/shard_map/ppermute | solution.py:277
  65.1 1.5 %collective-permute-start.16 = (s32[1032,128]{1,0:T(8,128)S(1)}, s32[1032,128]{1,0:T(8,128)S(1)}, u32[]{:S(2)}, u32[]{:S(2)}) collective-permute-start(s32[1032,128]{1,0:T(8,128)S(1)} %get-tuple-element.45), channel_id=1, source_target_pairs={{0,1},{1,0},{2,3},{3,2},{4,5},{5,4},{6,7},{7,6},{8,9},{9,8},{10,11... | collective-permute-start | bytes 1585160 | tf_op jit(solution)/shard_map/ppermute | solution.py:277
  66.7 1.5 %partial_sums.5 = s32[520,128]{1,0:T(8,128)S(1)} custom-call(s32[4,8]{1,0:T(4,128)S(1)} %copy-done.2, f32[2,1024,128]{2,1,0:T(8,128)S(1)} %get-tuple-element.48.kept, s32[1032,128]{1,0:T(8,128)S(1)} %collective-permute-done.9.received, bf16[2,1024,128]{2,1,0:T(8,128)(2,1)S(1)} %collective-permute-done.19.refs_0_, ...), custom_call_target="tpu_custom_call" | custom-call | flops 2097152 | bytes 3940480 | tf_op jit(solution)/shard_map/partial_sums/pallas_call | solution.py:83
  69.2 4.1 %collective-permute-done.18.refs_1_ = bf16[2,1024,128]{2,1,0:T(8,128)(2,1)S(1)} collective-permute-done((bf16[2,1024,128]{2,1,0:T(8,128)(2,1)}, bf16[2,1024,128]{2,1,0:T(8,128)(2,1)S(1)}, u32[]{:S(2)}, u32[]{:S(2)}) %collective-permute-start.18) | collective-permute-done | bytes 524320 | tf_op jit(solution)/shard_map/ppermute | solution.py:274
  73.3 8.3 %collective-permute-done.17.refs_1_ = s32[520,128]{1,0:T(8,128)S(1)} collective-permute-done((s32[520,128]{1,0:T(8,128)S(1)}, s32[520,128]{1,0:T(8,128)S(1)}, u32[]{:S(2)}, u32[]{:S(2)}) %collective-permute-start.17) | collective-permute-done | bytes 266272 | tf_op jit(solution)/shard_map/ppermute | solution.py:280
  (43 shorter events, 12.9 us)
Async XLA Ops:
  0.0 15.1 %collective-permute-start = (bf16[1024,256]{1,0:T(8,128)(2,1)}, bf16[1024,256]{1,0:T(8,128)(2,1)S(1)}, u32[]{:S(2)}, u32[]{:S(2)}) collective-permute-start(bf16[1024,256]{1,0:T(8,128)(2,1)} %refs_1_.1), channel_id=1, source_target_pairs={{0,16},{8,24},{16,0},{24,8},{1,17},{9,25},{17,1},{25,9},{2,18},{10... | collective-permute-start | bytes 1572872 | tf_op jit(solution)/shard_map/ppermute | solution.py:274
  2.9 15.5 %collective-permute-start.5 = (bf16[2,1024,128]{2,1,0:T(8,128)(2,1)}, bf16[2,1024,128]{2,1,0:T(8,128)(2,1)S(1)}, u32[]{:S(2)}, u32[]{:S(2)}) collective-permute-start(bf16[2,1024,128]{2,1,0:T(8,128)(2,1)} %refs_2_.1), channel_id=1, source_target_pairs={{0,2},{1,3},{2,4},{3,5},{4,6},{5,7},{6,0},{7,1},{8,10},{9,11},{10,... | collective-permute-start | bytes 1572872 | tf_op jit(solution)/shard_map/ppermute | solution.py:280
  4.5 14.4 %collective-permute-start.1 = (bf16[1024,256]{1,0:T(8,128)(2,1)}, bf16[1024,256]{1,0:T(8,128)(2,1)S(1)}, u32[]{:S(2)}, u32[]{:S(2)}) collective-permute-start(bf16[1024,256]{1,0:T(8,128)(2,1)} %refs_1_.1), channel_id=1, source_target_pairs={{0,8},{8,0},{16,24},{24,16},{1,9},{9,1},{17,25},{25,17},{2,10},{10... | collective-permute-start | bytes 1572872 | tf_op jit(solution)/shard_map/ppermute | solution.py:271
  15.1 11.8 %collective-permute-start.12 = (bf16[2,1024,128]{2,1,0:T(8,128)(2,1)}, bf16[2,1024,128]{2,1,0:T(8,128)(2,1)S(1)}, u32[]{:S(2)}, u32[]{:S(2)}) collective-permute-start(bf16[2,1024,128]{2,1,0:T(8,128)(2,1)} %refs_2_.1), channel_id=1, source_target_pairs={{0,8},{8,0},{16,24},{24,16},{1,9},{9,1},{17,25},{25,17},{2,10},{10... | collective-permute-start | bytes 1572872 | tf_op jit(solution)/shard_map/ppermute | solution.py:271
  18.4 12.5 %collective-permute-start.6 = (bf16[2,1024,128]{2,1,0:T(8,128)(2,1)S(1)}, bf16[2,1024,128]{2,1,0:T(8,128)(2,1)S(1)}, u32[]{:S(2)}, u32[]{:S(2)}) collective-permute-start(bf16[2,1024,128]{2,1,0:T(8,128)(2,1)S(1)} %collective-permute-done.5.refs_0_), channel_id=1, source_target_pairs={{0,16},{8,24},{16,0},{24,8},{1,17},{9,25},{17,1},{25,9},{2,18},{10... | collective-permute-start | bytes 1572872 | tf_op jit(solution)/shard_map/ppermute | solution.py:274
  18.9 14.3 %collective-permute-start.11 = (bf16[2,1024,128]{2,1,0:T(8,128)(2,1)S(1)}, bf16[2,1024,128]{2,1,0:T(8,128)(2,1)S(1)}, u32[]{:S(2)}, u32[]{:S(2)}) collective-permute-start(bf16[2,1024,128]{2,1,0:T(8,128)(2,1)S(1)} %collective-permute-done.5.refs_0_), channel_id=1, source_target_pairs={{0,2},{1,3},{2,4},{3,5},{4,6},{5,7},{6,0},{7,1},{8,10},{9,11},{10,... | collective-permute-start | bytes 1572872 | tf_op jit(solution)/shard_map/ppermute | solution.py:280
  20.5 14.5 %collective-permute-start.3 = (s32[1032,128]{1,0:T(8,128)S(1)}, s32[1032,128]{1,0:T(8,128)S(1)}, u32[]{:S(2)}, u32[]{:S(2)}) collective-permute-start(s32[1032,128]{1,0:T(8,128)S(1)} %get-tuple-element.35), channel_id=1, source_target_pairs={{0,1},{1,0},{2,3},{3,2},{4,5},{5,4},{6,7},{7,6},{8,9},{9,8},{10,11... | collective-permute-start | bytes 1585160 | tf_op jit(solution)/shard_map/ppermute | solution.py:277
  33.2 11.6 %collective-permute-start.13 = (bf16[2,1024,128]{2,1,0:T(8,128)(2,1)S(1)}, bf16[2,1024,128]{2,1,0:T(8,128)(2,1)S(1)}, u32[]{:S(2)}, u32[]{:S(2)}) collective-permute-start(bf16[2,1024,128]{2,1,0:T(8,128)(2,1)S(1)} %collective-permute-done.11.refs_0_), channel_id=1, source_target_pairs={{0,16},{8,24},{16,0},{24,8},{1,17},{9,25},{17,1},{25,9},{2,18},{10... | collective-permute-start | bytes 1572872 | tf_op jit(solution)/shard_map/ppermute | solution.py:274
  34.5 12.9 %collective-permute-start.19 = (bf16[2,1024,128]{2,1,0:T(8,128)(2,1)S(1)}, bf16[2,1024,128]{2,1,0:T(8,128)(2,1)S(1)}, u32[]{:S(2)}, u32[]{:S(2)}) collective-permute-start(bf16[2,1024,128]{2,1,0:T(8,128)(2,1)S(1)} %collective-permute-done.11.refs_0_), channel_id=1, source_target_pairs={{0,2},{1,3},{2,4},{3,5},{4,6},{5,7},{6,0},{7,1},{8,10},{9,11},{10,... | collective-permute-start | bytes 1572872 | tf_op jit(solution)/shard_map/ppermute | solution.py:280
  34.5 13.9 %collective-permute-start.7 = (bf16[2,1024,128]{2,1,0:T(8,128)(2,1)S(1)}, bf16[2,1024,128]{2,1,0:T(8,128)(2,1)S(1)}, u32[]{:S(2)}, u32[]{:S(2)}) collective-permute-start(bf16[2,1024,128]{2,1,0:T(8,128)(2,1)S(1)} %collective-permute-done.5.refs_0_), channel_id=1, source_target_pairs={{0,8},{8,0},{16,24},{24,16},{1,9},{9,1},{17,25},{25,17},{2,10},{10... | collective-permute-start | bytes 1572872 | tf_op jit(solution)/shard_map/ppermute | solution.py:271
  34.5 13.9 %collective-permute-start.8 = (bf16[2,1024,128]{2,1,0:T(8,128)(2,1)S(1)}, bf16[2,1024,128]{2,1,0:T(8,128)(2,1)S(1)}, u32[]{:S(2)}, u32[]{:S(2)}) collective-permute-start(bf16[2,1024,128]{2,1,0:T(8,128)(2,1)S(1)} %collective-permute-done.6.refs_1_), channel_id=1, source_target_pairs={{0,8},{8,0},{16,24},{24,16},{1,9},{9,1},{17,25},{25,17},{2,10},{10... | collective-permute-start | bytes 1572872 | tf_op jit(solution)/shard_map/ppermute | solution.py:271
  35.0 15.7 %collective-permute-start.4 = (s32[1032,128]{1,0:T(8,128)S(1)}, s32[1032,128]{1,0:T(8,128)S(1)}, u32[]{:S(2)}, u32[]{:S(2)}) collective-permute-start(s32[1032,128]{1,0:T(8,128)S(1)} %get-tuple-element.36), channel_id=1, source_target_pairs={{0,1},{1,0},{2,3},{3,2},{4,5},{5,4},{6,7},{7,6},{8,9},{9,8},{10,11... | collective-permute-start | bytes 1585160 | tf_op jit(solution)/shard_map/ppermute | solution.py:277
  47.3 10.1 %collective-permute-start.20 = (bf16[2,1024,128]{2,1,0:T(8,128)(2,1)S(1)}, bf16[2,1024,128]{2,1,0:T(8,128)(2,1)S(1)}, u32[]{:S(2)}, u32[]{:S(2)}) collective-permute-start(bf16[2,1024,128]{2,1,0:T(8,128)(2,1)S(1)} %collective-permute-done.19.refs_0_), channel_id=1, source_target_pairs={{0,16},{8,24},{16,0},{24,8},{1,17},{9,25},{17,1},{25,9},{2,18},{10... | collective-permute-start | bytes 1572872 | tf_op jit(solution)/shard_map/ppermute | solution.py:274
  49.9 8.9 %collective-permute-start.14 = (bf16[2,1024,128]{2,1,0:T(8,128)(2,1)S(1)}, bf16[2,1024,128]{2,1,0:T(8,128)(2,1)S(1)}, u32[]{:S(2)}, u32[]{:S(2)}) collective-permute-start(bf16[2,1024,128]{2,1,0:T(8,128)(2,1)S(1)} %collective-permute-done.11.refs_0_), channel_id=1, source_target_pairs={{0,8},{8,0},{16,24},{24,16},{1,9},{9,1},{17,25},{25,17},{2,10},{10... | collective-permute-start | bytes 1572872 | tf_op jit(solution)/shard_map/ppermute | solution.py:271
  50.0 8.8 %collective-permute-start.10 = (s32[520,128]{1,0:T(8,128)S(1)}, s32[520,128]{1,0:T(8,128)S(1)}, u32[]{:S(2)}, u32[]{:S(2)}) collective-permute-start(s32[520,128]{1,0:T(8,128)S(1)} %partial_sums.3), channel_id=1, source_target_pairs={{0,6},{1,7},{2,0},{3,1},{4,2},{5,3},{6,4},{7,5},{8,14},{9,15},{10,... | collective-permute-start | bytes 798728 | tf_op jit(solution)/shard_map/ppermute | solution.py:280
  50.7 9.0 %collective-permute-start.15 = (bf16[2,1024,128]{2,1,0:T(8,128)(2,1)S(1)}, bf16[2,1024,128]{2,1,0:T(8,128)(2,1)S(1)}, u32[]{:S(2)}, u32[]{:S(2)}) collective-permute-start(bf16[2,1024,128]{2,1,0:T(8,128)(2,1)S(1)} %collective-permute-done.13.refs_1_), channel_id=1, source_target_pairs={{0,8},{8,0},{16,24},{24,16},{1,9},{9,1},{17,25},{25,17},{2,10},{10... | collective-permute-start | bytes 1572872 | tf_op jit(solution)/shard_map/ppermute | solution.py:271
  50.7 14.4 %collective-permute-start.9 = (s32[1032,128]{1,0:T(8,128)S(1)}, s32[1032,128]{1,0:T(8,128)S(1)}, u32[]{:S(2)}, u32[]{:S(2)}) collective-permute-start(s32[1032,128]{1,0:T(8,128)S(1)} %get-tuple-element.39), channel_id=1, source_target_pairs={{0,1},{1,0},{2,3},{3,2},{4,5},{5,4},{6,7},{7,6},{8,9},{9,8},{10,11... | collective-permute-start | bytes 1585160 | tf_op jit(solution)/shard_map/ppermute | solution.py:277
  57.5 9.2 %collective-permute-start.21 = (bf16[2,1024,128]{2,1,0:T(8,128)(2,1)S(1)}, bf16[2,1024,128]{2,1,0:T(8,128)(2,1)S(1)}, u32[]{:S(2)}, u32[]{:S(2)}) collective-permute-start(bf16[2,1024,128]{2,1,0:T(8,128)(2,1)S(1)} %collective-permute-done.19.refs_0_), channel_id=1, source_target_pairs={{0,8},{8,0},{16,24},{24,16},{1,9},{9,1},{17,25},{25,17},{2,10},{10... | collective-permute-start | bytes 1572872 | tf_op jit(solution)/shard_map/ppermute | solution.py:271
  58.8 7.9 %collective-permute-start.22 = (bf16[2,1024,128]{2,1,0:T(8,128)(2,1)S(1)}, bf16[2,1024,128]{2,1,0:T(8,128)(2,1)S(1)}, u32[]{:S(2)}, u32[]{:S(2)}) collective-permute-start(bf16[2,1024,128]{2,1,0:T(8,128)(2,1)S(1)} %collective-permute-done.20.refs_1_), channel_id=1, source_target_pairs={{0,8},{8,0},{16,24},{24,16},{1,9},{9,1},{17,25},{25,17},{2,10},{10... | collective-permute-start | bytes 1572872 | tf_op jit(solution)/shard_map/ppermute | solution.py:271
  58.8 14.5 %collective-permute-start.18 = (bf16[2,1024,128]{2,1,0:T(8,128)(2,1)}, bf16[2,1024,128]{2,1,0:T(8,128)(2,1)S(1)}, u32[]{:S(2)}, u32[]{:S(2)}) collective-permute-start(bf16[2,1024,128]{2,1,0:T(8,128)(2,1)} %refs_2_.1), channel_id=1, source_target_pairs={{0,16},{8,24},{16,0},{24,8},{1,17},{9,25},{17,1},{25,9},{2,18},{10... | collective-permute-start | bytes 1572872 | tf_op jit(solution)/shard_map/ppermute | solution.py:274
  61.2 20.3 %collective-permute-start.17 = (s32[520,128]{1,0:T(8,128)S(1)}, s32[520,128]{1,0:T(8,128)S(1)}, u32[]{:S(2)}, u32[]{:S(2)}) collective-permute-start(s32[520,128]{1,0:T(8,128)S(1)} %partial_sums.4), channel_id=1, source_target_pairs={{0,4},{1,5},{2,6},{3,7},{4,0},{5,1},{6,2},{7,3},{8,12},{9,13},{10,... | collective-permute-start | bytes 798728 | tf_op jit(solution)/shard_map/ppermute | solution.py:280
  65.1 16.7 %collective-permute-start.16 = (s32[1032,128]{1,0:T(8,128)S(1)}, s32[1032,128]{1,0:T(8,128)S(1)}, u32[]{:S(2)}, u32[]{:S(2)}) collective-permute-start(s32[1032,128]{1,0:T(8,128)S(1)} %get-tuple-element.45), channel_id=1, source_target_pairs={{0,1},{1,0},{2,3},{3,2},{4,5},{5,4},{6,7},{7,6},{8,9},{9,8},{10,11... | collective-permute-start | bytes 1585160 | tf_op jit(solution)/shard_map/ppermute | solution.py:277
  68.2 14.9 %collective-permute-start.24 = (s32[520,128]{1,0:T(8,128)S(1)}, s32[520,128]{1,0:T(8,128)S(1)}, u32[]{:S(2)}, u32[]{:S(2)}) collective-permute-start(s32[520,128]{1,0:T(8,128)S(1)} %partial_sums.5), channel_id=1, source_target_pairs={{0,2},{1,3},{2,4},{3,5},{4,6},{5,7},{6,0},{7,1},{8,10},{9,11},{10,... | collective-permute-start | bytes 798728 | tf_op jit(solution)/shard_map/ppermute | solution.py:280
  73.3 8.5 %collective-permute-start.23 = (bf16[2,1024,128]{2,1,0:T(8,128)(2,1)S(1)}, bf16[2,1024,128]{2,1,0:T(8,128)(2,1)S(1)}, u32[]{:S(2)}, u32[]{:S(2)}) collective-permute-start(bf16[2,1024,128]{2,1,0:T(8,128)(2,1)S(1)} %collective-permute-done.18.refs_1_), channel_id=1, source_target_pairs={{0,8},{8,0},{16,24},{24,16},{1,9},{9,1},{17,25},{25,17},{2,10},{10... | collective-permute-start | bytes 1572872 | tf_op jit(solution)/shard_map/ppermute | solution.py:271
  (4 other events, 30.2 us)

commit v3 on v1

--- a/solution.py
+++ b/solution.py
@@ -37,7 +37,7 @@
 
 
 def encode(values):
-    largest = jnp.maximum(jnp.max(jnp.abs(values), axis=0, keepdims=True), 1e-30)
+    largest = jnp.maximum(jnp.max(jnp.abs(values), axis=0, keepdims=True), 1e-25)
     exponent = jnp.floor(jnp.log2(largest)) + 1.0
     share = values * (jnp.exp2(-exponent) * (TOP * TOP))
     root = share * lax.rsqrt(jnp.abs(share) + 1e-9)

time: 83.6 us -> 83.6 us (level)
  no operation moved by 1% of the time
where the time goes in v3:
time: 83.6 us; the launch traced here: 83.4 us
  waiting for transfers between devices  47.5 us (57%)
  starting transfers between devices  18.2 us (22%)
  Pallas kernels  14.4 us (17%)
  local copies, waits for them, and re-layouts  3.24 us (4%)
    ppermute x5, waiting for transfers between devices, along_chips(): lax.ppermute(value, 'out', [(r, (r + PAIR) % out_count) for r in range(ou...  27 us
    ppermute x6, waiting for transfers between devices, along_columns(): lax.ppermute(value, 'in', [(s, (s + PAIR * shift) % in_count) for s in ra...  16.9 us
    pallas_call x11, Pallas kernels, kernel_call(): pl.pallas_call(kernel, name=name, out_shape=outputs, in_specs=[pl.BlockSp...  14.4 us
    ppermute x5, starting transfers between devices, along_chips(): lax.ppermute(value, 'out', [(r, (r + PAIR) % out_count) for r in range(ou...  6.74 us
    ppermute x4, starting transfers between devices, across_sides(): return lax.ppermute(value, 'in', [(s, s ^ 1) for s in range(in_count)])  6.2 us
    ppermute x4, waiting for transfers between devices, across_sides(): return lax.ppermute(value, 'in', [(s, s ^ 1) for s in range(in_count)])  3.59 us
    ppermute x6, starting transfers between devices, along_columns(): lax.ppermute(value, 'in', [(s, (s + PAIR * shift) % in_count) for s in ra...  3.46 us
    unnamed x6, local copies, waits for them, and re-layouts  3.24 us
  transfers between devices with their start and end apart: 25, of which 11 were waited for; matrix products, arithmetic and copies ran while one was open for 0% of the time, Pallas kernels for 16%

profile of v3, /device:TPU:0, one launch (start us, length us, event | category | flops | bytes accessed | tf_op | source)
XLA Modules:
  0.0 83.4 jit_solution(7594494362245129487)
XLA Ops:
  0.0 2.9 %collective-permute-start = (bf16[1024,256]{1,0:T(8,128)(2,1)}, bf16[1024,256]{1,0:T(8,128)(2,1)S(1)}, u32[]{:S(2)}, u32[]{:S(2)}) collective-permute-start(bf16[1024,256]{1,0:T(8,128)(2,1)} %refs_1_.1), channel_id=1, source_target_pairs={{0,16},{8,24},{16,0},{24,8},{1,17},{9,25},{17,1},{25,9},{2,18},{10... | collective-permute-start | bytes 1572872 | tf_op jit(solution)/shard_map/ppermute | solution.py:274
  2.9 1.6 %collective-permute-start.5 = (bf16[2,1024,128]{2,1,0:T(8,128)(2,1)}, bf16[2,1024,128]{2,1,0:T(8,128)(2,1)S(1)}, u32[]{:S(2)}, u32[]{:S(2)}) collective-permute-start(bf16[2,1024,128]{2,1,0:T(8,128)(2,1)} %refs_2_.1), channel_id=1, source_target_pairs={{0,2},{1,3},{2,4},{3,5},{4,6},{5,7},{6,0},{7,1},{8,10},{9,11},{10,... | collective-permute-start | bytes 1572872 | tf_op jit(solution)/shard_map/ppermute | solution.py:280
  4.5 2.2 %copy-done = bf16[2,1024,1024]{2,1,0:T(8,128)(2,1)S(1)} copy-done((bf16[2,1024,1024]{2,1,0:T(8,128)(2,1)S(1)}, bf16[2,1024,1024]{2,1,0:T(8,128)(2,1)}, u32[]{:S(2)}) %copy-start) | copy-done | bytes 4194328
  9.1 5.9 %collective-permute-done.refs_1_ = bf16[1024,256]{1,0:T(8,128)(2,1)S(1)} collective-permute-done((bf16[1024,256]{1,0:T(8,128)(2,1)}, bf16[1024,256]{1,0:T(8,128)(2,1)S(1)}, u32[]{:S(2)}, u32[]{:S(2)}) %collective-permute-start) | collective-permute-done | bytes 524320 | tf_op jit(solution)/shard_map/ppermute | solution.py:274
  15.6 2.8 %collective-permute-done.5.refs_0_ = bf16[2,1024,128]{2,1,0:T(8,128)(2,1)S(1)} collective-permute-done((bf16[2,1024,128]{2,1,0:T(8,128)(2,1)}, bf16[2,1024,128]{2,1,0:T(8,128)(2,1)S(1)}, u32[]{:S(2)}, u32[]{:S(2)}) %collective-permute-start.5) | collective-permute-done | bytes 524320 | tf_op jit(solution)/shard_map/ppermute | solution.py:280
  18.9 1.6 %products.7 = (f32[2,1024,128]{2,1,0:T(8,128)S(1)}, s32[1032,128]{1,0:T(8,128)S(1)}) custom-call(bf16[2,1024,1024]{2,1,0:T(8,128)(2,1)S(1)} %get-tuple-element.27.weights, bf16[1024,256]{1,0:T(8,128)(2,1)S(1)} %get-tuple-element.28.refs_0_, bf16[1024,256]{1,0:T(8,128)(2,1)S(1)} %collective-permute-done.refs_1_, ...), custom_call_target="tpu_custom_call" | custom-call | flops 1073741824 | bytes 7868416 | tf_op jit(solution)/shard_map/products/pallas_call | solution.py:83
  20.5 1.6 %collective-permute-start.3 = (s32[1032,128]{1,0:T(8,128)S(1)}, s32[1032,128]{1,0:T(8,128)S(1)}, u32[]{:S(2)}, u32[]{:S(2)}) collective-permute-start(s32[1032,128]{1,0:T(8,128)S(1)} %get-tuple-element.34), channel_id=1, source_target_pairs={{0,1},{1,0},{2,3},{3,2},{4,5},{5,4},{6,7},{7,6},{8,9},{9,8},{10,11... | collective-permute-start | bytes 1585160 | tf_op jit(solution)/shard_map/ppermute | solution.py:277
  22.1 1.5 %products.4 = (f32[2,1024,128]{2,1,0:T(8,128)S(1)}, s32[1032,128]{1,0:T(8,128)S(1)}) custom-call(bf16[2,1024,1024]{2,1,0:T(8,128)(2,1)S(1)} %get-tuple-element.27.weights, bf16[1024,256]{1,0:T(8,128)(2,1)S(1)} %get-tuple-element.28.refs_0_, bf16[1024,256]{1,0:T(8,128)(2,1)S(1)} %collective-permute-done.refs_1_, ...), custom_call_target="tpu_custom_call" | custom-call | flops 1073741824 | bytes 7868416 | tf_op jit(solution)/shard_map/products/pallas_call | solution.py:83
  23.7 1.6 %products.5 = (f32[2,1024,128]{2,1,0:T(8,128)S(1)}, s32[1032,128]{1,0:T(8,128)S(1)}) custom-call(bf16[2,1024,1024]{2,1,0:T(8,128)(2,1)S(1)} %get-tuple-element.27.weights, bf16[1024,256]{1,0:T(8,128)(2,1)S(1)} %get-tuple-element.28.refs_0_, bf16[1024,256]{1,0:T(8,128)(2,1)S(1)} %collective-permute-done.refs_1_, ...), custom_call_target="tpu_custom_call" | custom-call | flops 1073741824 | bytes 7868416 | tf_op jit(solution)/shard_map/products/pallas_call | solution.py:83
  25.3 1.6 %products.6 = (f32[2,1024,128]{2,1,0:T(8,128)S(1)}, s32[1032,128]{1,0:T(8,128)S(1)}) custom-call(bf16[2,1024,1024]{2,1,0:T(8,128)(2,1)S(1)} %get-tuple-element.27.weights, bf16[1024,256]{1,0:T(8,128)(2,1)S(1)} %get-tuple-element.28.refs_0_, bf16[1024,256]{1,0:T(8,128)(2,1)S(1)} %collective-permute-done.refs_1_, ...), custom_call_target="tpu_custom_call" | custom-call | flops 1073741824 | bytes 7868416 | tf_op jit(solution)/shard_map/products/pallas_call | solution.py:83
  26.8 4.1 %collective-permute-done.6.refs_1_ = bf16[2,1024,128]{2,1,0:T(8,128)(2,1)S(1)} collective-permute-done((bf16[2,1024,128]{2,1,0:T(8,128)(2,1)S(1)}, bf16[2,1024,128]{2,1,0:T(8,128)(2,1)S(1)}, u32[]{:S(2)}, u32[]{:S(2)}) %collective-permute-start.6) | collective-permute-done | bytes 524320 | tf_op jit(solution)/shard_map/ppermute | solution.py:274
  30.9 2.3 %collective-permute-done.11.refs_0_ = bf16[2,1024,128]{2,1,0:T(8,128)(2,1)S(1)} collective-permute-done((bf16[2,1024,128]{2,1,0:T(8,128)(2,1)S(1)}, bf16[2,1024,128]{2,1,0:T(8,128)(2,1)S(1)}, u32[]{:S(2)}, u32[]{:S(2)}) %collective-permute-start.11) | collective-permute-done | bytes 524320 | tf_op jit(solution)/shard_map/ppermute | solution.py:280
  34.5 1.5 %collective-permute-start.4 = (s32[1032,128]{1,0:T(8,128)S(1)}, s32[1032,128]{1,0:T(8,128)S(1)}, u32[]{:S(2)}, u32[]{:S(2)}) collective-permute-start(s32[1032,128]{1,0:T(8,128)S(1)} %get-tuple-element.35), channel_id=1, source_target_pairs={{0,1},{1,0},{2,3},{3,2},{4,5},{5,4},{6,7},{7,6},{8,9},{9,8},{10,11... | collective-permute-start | bytes 1585160 | tf_op jit(solution)/shard_map/ppermute | solution.py:277
  36.5 8.3 %collective-permute-done.13.refs_1_ = bf16[2,1024,128]{2,1,0:T(8,128)(2,1)S(1)} collective-permute-done((bf16[2,1024,128]{2,1,0:T(8,128)(2,1)S(1)}, bf16[2,1024,128]{2,1,0:T(8,128)(2,1)S(1)}, u32[]{:S(2)}, u32[]{:S(2)}) %collective-permute-start.13) | collective-permute-done | bytes 524320 | tf_op jit(solution)/shard_map/ppermute | solution.py:274
  44.8 2.5 %collective-permute-done.19.refs_0_ = bf16[2,1024,128]{2,1,0:T(8,128)(2,1)S(1)} collective-permute-done((bf16[2,1024,128]{2,1,0:T(8,128)(2,1)S(1)}, bf16[2,1024,128]{2,1,0:T(8,128)(2,1)S(1)}, u32[]{:S(2)}, u32[]{:S(2)}) %collective-permute-start.19) | collective-permute-done | bytes 524320 | tf_op jit(solution)/shard_map/ppermute | solution.py:280
  48.4 1.5 %partial_sums.3 = s32[520,128]{1,0:T(8,128)S(1)} custom-call(s32[4,8]{1,0:T(4,128)S(1)} %copy-done.2, f32[2,1024,128]{2,1,0:T(8,128)S(1)} %get-tuple-element.36.kept, s32[1032,128]{1,0:T(8,128)S(1)} %collective-permute-done.3.received, bf16[2,1024,128]{2,1,0:T(8,128)(2,1)S(1)} %collective-permute-done.5.refs_0_, ...), custom_call_target="tpu_custom_call" | custom-call | flops 2097152 | bytes 3940480 | tf_op jit(solution)/shard_map/partial_sums/pallas_call | solution.py:83
  50.9 1.5 %collective-permute-start.9 = (s32[1032,128]{1,0:T(8,128)S(1)}, s32[1032,128]{1,0:T(8,128)S(1)}, u32[]{:S(2)}, u32[]{:S(2)}) collective-permute-start(s32[1032,128]{1,0:T(8,128)S(1)} %get-tuple-element.38), channel_id=1, source_target_pairs={{0,1},{1,0},{2,3},{3,2},{4,5},{5,4},{6,7},{7,6},{8,9},{9,8},{10,11... | collective-permute-start | bytes 1585160 | tf_op jit(solution)/shard_map/ppermute | solution.py:277
  52.4 5.1 %collective-permute-done.20.refs_1_ = bf16[2,1024,128]{2,1,0:T(8,128)(2,1)S(1)} collective-permute-done((bf16[2,1024,128]{2,1,0:T(8,128)(2,1)S(1)}, bf16[2,1024,128]{2,1,0:T(8,128)(2,1)S(1)}, u32[]{:S(2)}, u32[]{:S(2)}) %collective-permute-start.20) | collective-permute-done | bytes 524320 | tf_op jit(solution)/shard_map/ppermute | solution.py:274
  59.9 1.5 %partial_sums.4 = s32[520,128]{1,0:T(8,128)S(1)} custom-call(s32[4,8]{1,0:T(4,128)S(1)} %copy-done.2, f32[2,1024,128]{2,1,0:T(8,128)S(1)} %get-tuple-element.40.kept, s32[1032,128]{1,0:T(8,128)S(1)} %collective-permute-done.4.received, bf16[2,1024,128]{2,1,0:T(8,128)(2,1)S(1)} %collective-permute-done.11.refs_0_, ...), custom_call_target="tpu_custom_call" | custom-call | flops 2097152 | bytes 3940480 | tf_op jit(solution)/shard_map/partial_sums/pallas_call | solution.py:83
  61.5 3.6 %collective-permute-done.9.received = s32[1032,128]{1,0:T(8,128)S(1)} collective-permute-done((s32[1032,128]{1,0:T(8,128)S(1)}, s32[1032,128]{1,0:T(8,128)S(1)}, u32[]{:S(2)}, u32[]{:S(2)}) %collective-permute-start.9) | collective-permute-done | bytes 528416 | tf_op jit(solution)/shard_map/ppermute | solution.py:277
  65.1 1.5 %collective-permute-start.16 = (s32[1032,128]{1,0:T(8,128)S(1)}, s32[1032,128]{1,0:T(8,128)S(1)}, u32[]{:S(2)}, u32[]{:S(2)}) collective-permute-start(s32[1032,128]{1,0:T(8,128)S(1)} %get-tuple-element.43), channel_id=1, source_target_pairs={{0,1},{1,0},{2,3},{3,2},{4,5},{5,4},{6,7},{7,6},{8,9},{9,8},{10,11... | collective-permute-start | bytes 1585160 | tf_op jit(solution)/shard_map/ppermute | solution.py:277
  66.6 1.5 %partial_sums.5 = s32[520,128]{1,0:T(8,128)S(1)} custom-call(s32[4,8]{1,0:T(4,128)S(1)} %copy-done.2, f32[2,1024,128]{2,1,0:T(8,128)S(1)} %get-tuple-element.46.kept, s32[1032,128]{1,0:T(8,128)S(1)} %collective-permute-done.9.received, bf16[2,1024,128]{2,1,0:T(8,128)(2,1)S(1)} %collective-permute-done.19.refs_0_, ...), custom_call_target="tpu_custom_call" | custom-call | flops 2097152 | bytes 3940480 | tf_op jit(solution)/shard_map/partial_sums/pallas_call | solution.py:83
  69.2 3.5 %collective-permute-done.18.refs_1_ = bf16[2,1024,128]{2,1,0:T(8,128)(2,1)S(1)} collective-permute-done((bf16[2,1024,128]{2,1,0:T(8,128)(2,1)}, bf16[2,1024,128]{2,1,0:T(8,128)(2,1)S(1)}, u32[]{:S(2)}, u32[]{:S(2)}) %collective-permute-start.18) | collective-permute-done | bytes 524320 | tf_op jit(solution)/shard_map/ppermute | solution.py:274
  72.7 8.4 %collective-permute-done.17.refs_1_ = s32[520,128]{1,0:T(8,128)S(1)} collective-permute-done((s32[520,128]{1,0:T(8,128)S(1)}, s32[520,128]{1,0:T(8,128)S(1)}, u32[]{:S(2)}, u32[]{:S(2)}) %collective-permute-start.17) | collective-permute-done | bytes 266272 | tf_op jit(solution)/shard_map/ppermute | solution.py:280
  (43 shorter events, 13.2 us)
Async XLA Ops:
  0.0 15.1 %collective-permute-start = (bf16[1024,256]{1,0:T(8,128)(2,1)}, bf16[1024,256]{1,0:T(8,128)(2,1)S(1)}, u32[]{:S(2)}, u32[]{:S(2)}) collective-permute-start(bf16[1024,256]{1,0:T(8,128)(2,1)} %refs_1_.1), channel_id=1, source_target_pairs={{0,16},{8,24},{16,0},{24,8},{1,17},{9,25},{17,1},{25,9},{2,18},{10... | collective-permute-start | bytes 1572872 | tf_op jit(solution)/shard_map/ppermute | solution.py:274
  2.9 15.5 %collective-permute-start.5 = (bf16[2,1024,128]{2,1,0:T(8,128)(2,1)}, bf16[2,1024,128]{2,1,0:T(8,128)(2,1)S(1)}, u32[]{:S(2)}, u32[]{:S(2)}) collective-permute-start(bf16[2,1024,128]{2,1,0:T(8,128)(2,1)} %refs_2_.1), channel_id=1, source_target_pairs={{0,2},{1,3},{2,4},{3,5},{4,6},{5,7},{6,0},{7,1},{8,10},{9,11},{10,... | collective-permute-start | bytes 1572872 | tf_op jit(solution)/shard_map/ppermute | solution.py:280
  4.5 14.4 %collective-permute-start.1 = (bf16[1024,256]{1,0:T(8,128)(2,1)}, bf16[1024,256]{1,0:T(8,128)(2,1)S(1)}, u32[]{:S(2)}, u32[]{:S(2)}) collective-permute-start(bf16[1024,256]{1,0:T(8,128)(2,1)} %refs_1_.1), channel_id=1, source_target_pairs={{0,8},{8,0},{16,24},{24,16},{1,9},{9,1},{17,25},{25,17},{2,10},{10... | collective-permute-start | bytes 1572872 | tf_op jit(solution)/shard_map/ppermute | solution.py:271
  15.1 11.8 %collective-permute-start.12 = (bf16[2,1024,128]{2,1,0:T(8,128)(2,1)}, bf16[2,1024,128]{2,1,0:T(8,128)(2,1)S(1)}, u32[]{:S(2)}, u32[]{:S(2)}) collective-permute-start(bf16[2,1024,128]{2,1,0:T(8,128)(2,1)} %refs_2_.1), channel_id=1, source_target_pairs={{0,8},{8,0},{16,24},{24,16},{1,9},{9,1},{17,25},{25,17},{2,10},{10... | collective-permute-start | bytes 1572872 | tf_op jit(solution)/shard_map/ppermute | solution.py:271
  18.4 12.5 %collective-permute-start.6 = (bf16[2,1024,128]{2,1,0:T(8,128)(2,1)S(1)}, bf16[2,1024,128]{2,1,0:T(8,128)(2,1)S(1)}, u32[]{:S(2)}, u32[]{:S(2)}) collective-permute-start(bf16[2,1024,128]{2,1,0:T(8,128)(2,1)S(1)} %collective-permute-done.5.refs_0_), channel_id=1, source_target_pairs={{0,16},{8,24},{16,0},{24,8},{1,17},{9,25},{17,1},{25,9},{2,18},{10... | collective-permute-start | bytes 1572872 | tf_op jit(solution)/shard_map/ppermute | solution.py:274
  18.9 14.3 %collective-permute-start.11 = (bf16[2,1024,128]{2,1,0:T(8,128)(2,1)S(1)}, bf16[2,1024,128]{2,1,0:T(8,128)(2,1)S(1)}, u32[]{:S(2)}, u32[]{:S(2)}) collective-permute-start(bf16[2,1024,128]{2,1,0:T(8,128)(2,1)S(1)} %collective-permute-done.5.refs_0_), channel_id=1, source_target_pairs={{0,2},{1,3},{2,4},{3,5},{4,6},{5,7},{6,0},{7,1},{8,10},{9,11},{10,... | collective-permute-start | bytes 1572872 | tf_op jit(solution)/shard_map/ppermute | solution.py:280
  20.5 14.0 %collective-permute-start.3 = (s32[1032,128]{1,0:T(8,128)S(1)}, s32[1032,128]{1,0:T(8,128)S(1)}, u32[]{:S(2)}, u32[]{:S(2)}) collective-permute-start(s32[1032,128]{1,0:T(8,128)S(1)} %get-tuple-element.34), channel_id=1, source_target_pairs={{0,1},{1,0},{2,3},{3,2},{4,5},{5,4},{6,7},{7,6},{8,9},{9,8},{10,11... | collective-permute-start | bytes 1585160 | tf_op jit(solution)/shard_map/ppermute | solution.py:277
  33.2 11.6 %collective-permute-start.13 = (bf16[2,1024,128]{2,1,0:T(8,128)(2,1)S(1)}, bf16[2,1024,128]{2,1,0:T(8,128)(2,1)S(1)}, u32[]{:S(2)}, u32[]{:S(2)}) collective-permute-start(bf16[2,1024,128]{2,1,0:T(8,128)(2,1)S(1)} %collective-permute-done.11.refs_0_), channel_id=1, source_target_pairs={{0,16},{8,24},{16,0},{24,8},{1,17},{9,25},{17,1},{25,9},{2,18},{10... | collective-permute-start | bytes 1572872 | tf_op jit(solution)/shard_map/ppermute | solution.py:274
  34.5 12.9 %collective-permute-start.19 = (bf16[2,1024,128]{2,1,0:T(8,128)(2,1)S(1)}, bf16[2,1024,128]{2,1,0:T(8,128)(2,1)S(1)}, u32[]{:S(2)}, u32[]{:S(2)}) collective-permute-start(bf16[2,1024,128]{2,1,0:T(8,128)(2,1)S(1)} %collective-permute-done.11.refs_0_), channel_id=1, source_target_pairs={{0,2},{1,3},{2,4},{3,5},{4,6},{5,7},{6,0},{7,1},{8,10},{9,11},{10,... | collective-permute-start | bytes 1572872 | tf_op jit(solution)/shard_map/ppermute | solution.py:280
  34.5 16.2 %collective-permute-start.4 = (s32[1032,128]{1,0:T(8,128)S(1)}, s32[1032,128]{1,0:T(8,128)S(1)}, u32[]{:S(2)}, u32[]{:S(2)}) collective-permute-start(s32[1032,128]{1,0:T(8,128)S(1)} %get-tuple-element.35), channel_id=1, source_target_pairs={{0,1},{1,0},{2,3},{3,2},{4,5},{5,4},{6,7},{7,6},{8,9},{9,8},{10,11... | collective-permute-start | bytes 1585160 | tf_op jit(solution)/shard_map/ppermute | solution.py:277
  36.0 12.4 %collective-permute-start.7 = (bf16[2,1024,128]{2,1,0:T(8,128)(2,1)S(1)}, bf16[2,1024,128]{2,1,0:T(8,128)(2,1)S(1)}, u32[]{:S(2)}, u32[]{:S(2)}) collective-permute-start(bf16[2,1024,128]{2,1,0:T(8,128)(2,1)S(1)} %collective-permute-done.5.refs_0_), channel_id=1, source_target_pairs={{0,8},{8,0},{16,24},{24,16},{1,9},{9,1},{17,25},{25,17},{2,10},{10... | collective-permute-start | bytes 1572872 | tf_op jit(solution)/shard_map/ppermute | solution.py:271
  36.0 12.4 %collective-permute-start.8 = (bf16[2,1024,128]{2,1,0:T(8,128)(2,1)S(1)}, bf16[2,1024,128]{2,1,0:T(8,128)(2,1)S(1)}, u32[]{:S(2)}, u32[]{:S(2)}) collective-permute-start(bf16[2,1024,128]{2,1,0:T(8,128)(2,1)S(1)} %collective-permute-done.6.refs_1_), channel_id=1, source_target_pairs={{0,8},{8,0},{16,24},{24,16},{1,9},{9,1},{17,25},{25,17},{2,10},{10... | collective-permute-start | bytes 1572872 | tf_op jit(solution)/shard_map/ppermute | solution.py:271
  47.3 10.1 %collective-permute-start.20 = (bf16[2,1024,128]{2,1,0:T(8,128)(2,1)S(1)}, bf16[2,1024,128]{2,1,0:T(8,128)(2,1)S(1)}, u32[]{:S(2)}, u32[]{:S(2)}) collective-permute-start(bf16[2,1024,128]{2,1,0:T(8,128)(2,1)S(1)} %collective-permute-done.19.refs_0_), channel_id=1, source_target_pairs={{0,16},{8,24},{16,0},{24,8},{1,17},{9,25},{17,1},{25,9},{2,18},{10... | collective-permute-start | bytes 1572872 | tf_op jit(solution)/shard_map/ppermute | solution.py:274
  48.4 9.1 %collective-permute-start.14 = (bf16[2,1024,128]{2,1,0:T(8,128)(2,1)S(1)}, bf16[2,1024,128]{2,1,0:T(8,128)(2,1)S(1)}, u32[]{:S(2)}, u32[]{:S(2)}) collective-permute-start(bf16[2,1024,128]{2,1,0:T(8,128)(2,1)S(1)} %collective-permute-done.11.refs_0_), channel_id=1, source_target_pairs={{0,8},{8,0},{16,24},{24,16},{1,9},{9,1},{17,25},{25,17},{2,10},{10... | collective-permute-start | bytes 1572872 | tf_op jit(solution)/shard_map/ppermute | solution.py:271
  49.9 9.0 %collective-permute-start.10 = (s32[520,128]{1,0:T(8,128)S(1)}, s32[520,128]{1,0:T(8,128)S(1)}, u32[]{:S(2)}, u32[]{:S(2)}) collective-permute-start(s32[520,128]{1,0:T(8,128)S(1)} %partial_sums.3), channel_id=1, source_target_pairs={{0,6},{1,7},{2,0},{3,1},{4,2},{5,3},{6,4},{7,5},{8,14},{9,15},{10,... | collective-permute-start | bytes 798728 | tf_op jit(solution)/shard_map/ppermute | solution.py:280
  50.6 9.3 %collective-permute-start.15 = (bf16[2,1024,128]{2,1,0:T(8,128)(2,1)S(1)}, bf16[2,1024,128]{2,1,0:T(8,128)(2,1)S(1)}, u32[]{:S(2)}, u32[]{:S(2)}) collective-permute-start(bf16[2,1024,128]{2,1,0:T(8,128)(2,1)S(1)} %collective-permute-done.13.refs_1_), channel_id=1, source_target_pairs={{0,8},{8,0},{16,24},{24,16},{1,9},{9,1},{17,25},{25,17},{2,10},{10... | collective-permute-start | bytes 1572872 | tf_op jit(solution)/shard_map/ppermute | solution.py:271
  50.9 14.2 %collective-permute-start.9 = (s32[1032,128]{1,0:T(8,128)S(1)}, s32[1032,128]{1,0:T(8,128)S(1)}, u32[]{:S(2)}, u32[]{:S(2)}) collective-permute-start(s32[1032,128]{1,0:T(8,128)S(1)} %get-tuple-element.38), channel_id=1, source_target_pairs={{0,1},{1,0},{2,3},{3,2},{4,5},{5,4},{6,7},{7,6},{8,9},{9,8},{10,11... | collective-permute-start | bytes 1585160 | tf_op jit(solution)/shard_map/ppermute | solution.py:277
  57.5 9.1 %collective-permute-start.21 = (bf16[2,1024,128]{2,1,0:T(8,128)(2,1)S(1)}, bf16[2,1024,128]{2,1,0:T(8,128)(2,1)S(1)}, u32[]{:S(2)}, u32[]{:S(2)}) collective-permute-start(bf16[2,1024,128]{2,1,0:T(8,128)(2,1)S(1)} %collective-permute-done.19.refs_0_), channel_id=1, source_target_pairs={{0,8},{8,0},{16,24},{24,16},{1,9},{9,1},{17,25},{25,17},{2,10},{10... | collective-permute-start | bytes 1572872 | tf_op jit(solution)/shard_map/ppermute | solution.py:271
  57.5 9.1 %collective-permute-start.22 = (bf16[2,1024,128]{2,1,0:T(8,128)(2,1)S(1)}, bf16[2,1024,128]{2,1,0:T(8,128)(2,1)S(1)}, u32[]{:S(2)}, u32[]{:S(2)}) collective-permute-start(bf16[2,1024,128]{2,1,0:T(8,128)(2,1)S(1)} %collective-permute-done.20.refs_1_), channel_id=1, source_target_pairs={{0,8},{8,0},{16,24},{24,16},{1,9},{9,1},{17,25},{25,17},{2,10},{10... | collective-permute-start | bytes 1572872 | tf_op jit(solution)/shard_map/ppermute | solution.py:271
  58.9 13.8 %collective-permute-start.18 = (bf16[2,1024,128]{2,1,0:T(8,128)(2,1)}, bf16[2,1024,128]{2,1,0:T(8,128)(2,1)S(1)}, u32[]{:S(2)}, u32[]{:S(2)}) collective-permute-start(bf16[2,1024,128]{2,1,0:T(8,128)(2,1)} %refs_2_.1), channel_id=1, source_target_pairs={{0,16},{8,24},{16,0},{24,8},{1,17},{9,25},{17,1},{25,9},{2,18},{10... | collective-permute-start | bytes 1572872 | tf_op jit(solution)/shard_map/ppermute | solution.py:274
  61.4 19.6 %collective-permute-start.17 = (s32[520,128]{1,0:T(8,128)S(1)}, s32[520,128]{1,0:T(8,128)S(1)}, u32[]{:S(2)}, u32[]{:S(2)}) collective-permute-start(s32[520,128]{1,0:T(8,128)S(1)} %partial_sums.4), channel_id=1, source_target_pairs={{0,4},{1,5},{2,6},{3,7},{4,0},{5,1},{6,2},{7,3},{8,12},{9,13},{10,... | collective-permute-start | bytes 798728 | tf_op jit(solution)/shard_map/ppermute | solution.py:280
  65.1 16.2 %collective-permute-start.16 = (s32[1032,128]{1,0:T(8,128)S(1)}, s32[1032,128]{1,0:T(8,128)S(1)}, u32[]{:S(2)}, u32[]{:S(2)}) collective-permute-start(s32[1032,128]{1,0:T(8,128)S(1)} %get-tuple-element.43), channel_id=1, source_target_pairs={{0,1},{1,0},{2,3},{3,2},{4,5},{5,4},{6,7},{7,6},{8,9},{9,8},{10,11... | collective-permute-start | bytes 1585160 | tf_op jit(solution)/shard_map/ppermute | solution.py:277
  68.1 14.5 %collective-permute-start.24 = (s32[520,128]{1,0:T(8,128)S(1)}, s32[520,128]{1,0:T(8,128)S(1)}, u32[]{:S(2)}, u32[]{:S(2)}) collective-permute-start(s32[520,128]{1,0:T(8,128)S(1)} %partial_sums.5), channel_id=1, source_target_pairs={{0,2},{1,3},{2,4},{3,5},{4,6},{5,7},{6,0},{7,1},{8,10},{9,11},{10,... | collective-permute-start | bytes 798728 | tf_op jit(solution)/shard_map/ppermute | solution.py:280
  72.7 8.6 %collective-permute-start.23 = (bf16[2,1024,128]{2,1,0:T(8,128)(2,1)S(1)}, bf16[2,1024,128]{2,1,0:T(8,128)(2,1)S(1)}, u32[]{:S(2)}, u32[]{:S(2)}) collective-permute-start(bf16[2,1024,128]{2,1,0:T(8,128)(2,1)S(1)} %collective-permute-done.18.refs_1_), channel_id=1, source_target_pairs={{0,8},{8,0},{16,24},{24,16},{1,9},{9,1},{17,25},{25,17},{2,10},{10... | collective-permute-start | bytes 1572872 | tf_op jit(solution)/shard_map/ppermute | solution.py:271
  (4 other events, 30.2 us)

commit v4 on v3

--- a/solution.py
+++ b/solution.py
@@ -310,7 +310,7 @@
         return partial
 
     for place, step in enumerate(order):
-        earlier = [received[order[place - 1]]] if place > 0 else []
+        earlier = [received[order[place - (2 if place == columns - 1 else 1)]]] if place > 0 else []
         if place > 1:
             earlier.append(send_sums(place - 2))
         received[step] = near(across_sides(after(sent[step], *earlier)))

time: 83.6 us -> 83.6 us (level)
    ppermute x4, waiting for transfers between devices: 3.59 us -> 2.62 us  [across_sides(): return lax.ppermute(value, 'in', [(s, s ^ 1) for s in range(in_count)])]
where the time goes in v4:
time: 83.6 us; the launch traced here: 83.4 us
  waiting for transfers between devices  47 us (56%)
  starting transfers between devices  18.7 us (22%)
  Pallas kernels  14.4 us (17%)
  local copies, waits for them, and re-layouts  3.24 us (4%)
    ppermute x5, waiting for transfers between devices, along_chips(): lax.ppermute(value, 'out', [(r, (r + PAIR) % out_count) for r in range(ou...  27.4 us
    ppermute x6, waiting for transfers between devices, along_columns(): lax.ppermute(value, 'in', [(s, (s + PAIR * shift) % in_count) for s in ra...  16.9 us
    pallas_call x11, Pallas kernels, kernel_call(): pl.pallas_call(kernel, name=name, out_shape=outputs, in_specs=[pl.BlockSp...  14.4 us
    ppermute x5, starting transfers between devices, along_chips(): lax.ppermute(value, 'out', [(r, (r + PAIR) % out_count) for r in range(ou...  6.74 us
    ppermute x4, starting transfers between devices, across_sides(): return lax.ppermute(value, 'in', [(s, s ^ 1) for s in range(in_count)])  6.27 us
    ppermute x6, starting transfers between devices, along_columns(): lax.ppermute(value, 'in', [(s, (s + PAIR * shift) % in_count) for s in ra...  3.89 us
    unnamed x6, local copies, waits for them, and re-layouts  3.24 us
    ppermute x4, waiting for transfers between devices, across_sides(): return lax.ppermute(value, 'in', [(s, s ^ 1) for s in range(in_count)])  2.62 us
  transfers between devices with their start and end apart: 25, of which 11 were waited for; matrix products, arithmetic and copies ran while one was open for 0% of the time, Pallas kernels for 16%

profile of v4, /device:TPU:0, one launch (start us, length us, event | category | flops | bytes accessed | tf_op | source)
XLA Modules:
  0.0 83.4 jit_solution(509541201311380882)
XLA Ops:
  0.0 2.9 %collective-permute-start = (bf16[1024,256]{1,0:T(8,128)(2,1)}, bf16[1024,256]{1,0:T(8,128)(2,1)S(1)}, u32[]{:S(2)}, u32[]{:S(2)}) collective-permute-start(bf16[1024,256]{1,0:T(8,128)(2,1)} %refs_1_.1), channel_id=1, source_target_pairs={{0,16},{8,24},{16,0},{24,8},{1,17},{9,25},{17,1},{25,9},{2,18},{10... | collective-permute-start | bytes 1572872 | tf_op jit(solution)/shard_map/ppermute | solution.py:274
  2.9 1.6 %collective-permute-start.5 = (bf16[2,1024,128]{2,1,0:T(8,128)(2,1)}, bf16[2,1024,128]{2,1,0:T(8,128)(2,1)S(1)}, u32[]{:S(2)}, u32[]{:S(2)}) collective-permute-start(bf16[2,1024,128]{2,1,0:T(8,128)(2,1)} %refs_2_.1), channel_id=1, source_target_pairs={{0,2},{1,3},{2,4},{3,5},{4,6},{5,7},{6,0},{7,1},{8,10},{9,11},{10,... | collective-permute-start | bytes 1572872 | tf_op jit(solution)/shard_map/ppermute | solution.py:280
  4.5 2.2 %copy-done = bf16[2,1024,1024]{2,1,0:T(8,128)(2,1)S(1)} copy-done((bf16[2,1024,1024]{2,1,0:T(8,128)(2,1)S(1)}, bf16[2,1024,1024]{2,1,0:T(8,128)(2,1)}, u32[]{:S(2)}) %copy-start) | copy-done | bytes 4194328
  9.1 5.9 %collective-permute-done.refs_1_ = bf16[1024,256]{1,0:T(8,128)(2,1)S(1)} collective-permute-done((bf16[1024,256]{1,0:T(8,128)(2,1)}, bf16[1024,256]{1,0:T(8,128)(2,1)S(1)}, u32[]{:S(2)}, u32[]{:S(2)}) %collective-permute-start) | collective-permute-done | bytes 524320 | tf_op jit(solution)/shard_map/ppermute | solution.py:274
  15.6 2.8 %collective-permute-done.5.refs_0_ = bf16[2,1024,128]{2,1,0:T(8,128)(2,1)S(1)} collective-permute-done((bf16[2,1024,128]{2,1,0:T(8,128)(2,1)}, bf16[2,1024,128]{2,1,0:T(8,128)(2,1)S(1)}, u32[]{:S(2)}, u32[]{:S(2)}) %collective-permute-start.5) | collective-permute-done | bytes 524320 | tf_op jit(solution)/shard_map/ppermute | solution.py:280
  18.9 1.6 %products.6 = (f32[2,1024,128]{2,1,0:T(8,128)S(1)}, s32[1032,128]{1,0:T(8,128)S(1)}) custom-call(bf16[2,1024,1024]{2,1,0:T(8,128)(2,1)S(1)} %get-tuple-element.27.weights, bf16[1024,256]{1,0:T(8,128)(2,1)S(1)} %get-tuple-element.28.refs_0_, bf16[1024,256]{1,0:T(8,128)(2,1)S(1)} %collective-permute-done.refs_1_, ...), custom_call_target="tpu_custom_call" | custom-call | flops 1073741824 | bytes 7868416 | tf_op jit(solution)/shard_map/products/pallas_call | solution.py:83
  20.5 1.6 %collective-permute-start.3 = (s32[1032,128]{1,0:T(8,128)S(1)}, s32[1032,128]{1,0:T(8,128)S(1)}, u32[]{:S(2)}, u32[]{:S(2)}) collective-permute-start(s32[1032,128]{1,0:T(8,128)S(1)} %get-tuple-element.33), channel_id=1, source_target_pairs={{0,1},{1,0},{2,3},{3,2},{4,5},{5,4},{6,7},{7,6},{8,9},{9,8},{10,11... | collective-permute-start | bytes 1585160 | tf_op jit(solution)/shard_map/ppermute | solution.py:277
  22.1 1.5 %products.5 = (f32[2,1024,128]{2,1,0:T(8,128)S(1)}, s32[1032,128]{1,0:T(8,128)S(1)}) custom-call(bf16[2,1024,1024]{2,1,0:T(8,128)(2,1)S(1)} %get-tuple-element.27.weights, bf16[1024,256]{1,0:T(8,128)(2,1)S(1)} %get-tuple-element.28.refs_0_, bf16[1024,256]{1,0:T(8,128)(2,1)S(1)} %collective-permute-done.refs_1_, ...), custom_call_target="tpu_custom_call" | custom-call | flops 1073741824 | bytes 7868416 | tf_op jit(solution)/shard_map/products/pallas_call | solution.py:83
  23.7 1.6 %products.7 = (f32[2,1024,128]{2,1,0:T(8,128)S(1)}, s32[1032,128]{1,0:T(8,128)S(1)}) custom-call(bf16[2,1024,1024]{2,1,0:T(8,128)(2,1)S(1)} %get-tuple-element.27.weights, bf16[1024,256]{1,0:T(8,128)(2,1)S(1)} %get-tuple-element.28.refs_0_, bf16[1024,256]{1,0:T(8,128)(2,1)S(1)} %collective-permute-done.refs_1_, ...), custom_call_target="tpu_custom_call" | custom-call | flops 1073741824 | bytes 7868416 | tf_op jit(solution)/shard_map/products/pallas_call | solution.py:83
  25.3 1.6 %products.4 = (f32[2,1024,128]{2,1,0:T(8,128)S(1)}, s32[1032,128]{1,0:T(8,128)S(1)}) custom-call(bf16[2,1024,1024]{2,1,0:T(8,128)(2,1)S(1)} %get-tuple-element.27.weights, bf16[1024,256]{1,0:T(8,128)(2,1)S(1)} %get-tuple-element.28.refs_0_, bf16[1024,256]{1,0:T(8,128)(2,1)S(1)} %collective-permute-done.refs_1_, ...), custom_call_target="tpu_custom_call" | custom-call | flops 1073741824 | bytes 7868416 | tf_op jit(solution)/shard_map/products/pallas_call | solution.py:83
  26.8 4.1 %collective-permute-done.6.refs_1_ = bf16[2,1024,128]{2,1,0:T(8,128)(2,1)S(1)} collective-permute-done((bf16[2,1024,128]{2,1,0:T(8,128)(2,1)S(1)}, bf16[2,1024,128]{2,1,0:T(8,128)(2,1)S(1)}, u32[]{:S(2)}, u32[]{:S(2)}) %collective-permute-start.6) | collective-permute-done | bytes 524320 | tf_op jit(solution)/shard_map/ppermute | solution.py:274
  30.9 2.3 %collective-permute-done.10.refs_0_ = bf16[2,1024,128]{2,1,0:T(8,128)(2,1)S(1)} collective-permute-done((bf16[2,1024,128]{2,1,0:T(8,128)(2,1)S(1)}, bf16[2,1024,128]{2,1,0:T(8,128)(2,1)S(1)}, u32[]{:S(2)}, u32[]{:S(2)}) %collective-permute-start.10) | collective-permute-done | bytes 524320 | tf_op jit(solution)/shard_map/ppermute | solution.py:280
  34.5 1.5 %collective-permute-start.4 = (s32[1032,128]{1,0:T(8,128)S(1)}, s32[1032,128]{1,0:T(8,128)S(1)}, u32[]{:S(2)}, u32[]{:S(2)}) collective-permute-start(s32[1032,128]{1,0:T(8,128)S(1)} %get-tuple-element.34), channel_id=1, source_target_pairs={{0,1},{1,0},{2,3},{3,2},{4,5},{5,4},{6,7},{7,6},{8,9},{9,8},{10,11... | collective-permute-start | bytes 1585160 | tf_op jit(solution)/shard_map/ppermute | solution.py:277
  36.5 8.3 %collective-permute-done.12.refs_1_ = bf16[2,1024,128]{2,1,0:T(8,128)(2,1)S(1)} collective-permute-done((bf16[2,1024,128]{2,1,0:T(8,128)(2,1)S(1)}, bf16[2,1024,128]{2,1,0:T(8,128)(2,1)S(1)}, u32[]{:S(2)}, u32[]{:S(2)}) %collective-permute-start.12) | collective-permute-done | bytes 524320 | tf_op jit(solution)/shard_map/ppermute | solution.py:274
  44.8 2.5 %collective-permute-done.19.refs_0_ = bf16[2,1024,128]{2,1,0:T(8,128)(2,1)S(1)} collective-permute-done((bf16[2,1024,128]{2,1,0:T(8,128)(2,1)S(1)}, bf16[2,1024,128]{2,1,0:T(8,128)(2,1)S(1)}, u32[]{:S(2)}, u32[]{:S(2)}) %collective-permute-start.19) | collective-permute-done | bytes 524320 | tf_op jit(solution)/shard_map/ppermute | solution.py:280
  50.9 1.5 %collective-permute-start.18 = (s32[1032,128]{1,0:T(8,128)S(1)}, s32[1032,128]{1,0:T(8,128)S(1)}, u32[]{:S(2)}, u32[]{:S(2)}) collective-permute-start(s32[1032,128]{1,0:T(8,128)S(1)} %get-tuple-element.46), channel_id=1, source_target_pairs={{0,1},{1,0},{2,3},{3,2},{4,5},{5,4},{6,7},{7,6},{8,9},{9,8},{10,11... | collective-permute-start | bytes 1585160 | tf_op jit(solution)/shard_map/ppermute | solution.py:277
  52.4 5.1 %collective-permute-done.20.refs_1_ = bf16[2,1024,128]{2,1,0:T(8,128)(2,1)S(1)} collective-permute-done((bf16[2,1024,128]{2,1,0:T(8,128)(2,1)S(1)}, bf16[2,1024,128]{2,1,0:T(8,128)(2,1)S(1)}, u32[]{:S(2)}, u32[]{:S(2)}) %collective-permute-start.20) | collective-permute-done | bytes 524320 | tf_op jit(solution)/shard_map/ppermute | solution.py:274
  59.9 1.5 %partial_sums.4 = s32[520,128]{1,0:T(8,128)S(1)} custom-call(s32[4,8]{1,0:T(4,128)S(1)} %copy-done.2, f32[2,1024,128]{2,1,0:T(8,128)S(1)} %get-tuple-element.38.kept, s32[1032,128]{1,0:T(8,128)S(1)} %collective-permute-done.4.received, bf16[2,1024,128]{2,1,0:T(8,128)(2,1)S(1)} %collective-permute-done.10.refs_0_, ...), custom_call_target="tpu_custom_call" | custom-call | flops 2097152 | bytes 3940480 | tf_op jit(solution)/shard_map/partial_sums/pallas_call | solution.py:83
  61.5 1.6 %collective-permute-start.15 = (s32[1032,128]{1,0:T(8,128)S(1)}, s32[1032,128]{1,0:T(8,128)S(1)}, u32[]{:S(2)}, u32[]{:S(2)}) collective-permute-start(s32[1032,128]{1,0:T(8,128)S(1)} %get-tuple-element.42), channel_id=1, source_target_pairs={{0,1},{1,0},{2,3},{3,2},{4,5},{5,4},{6,7},{7,6},{8,9},{9,8},{10,11... | collective-permute-start | bytes 1585160 | tf_op jit(solution)/shard_map/ppermute | solution.py:277
  63.1 2.6 %collective-permute-done.18.received = s32[1032,128]{1,0:T(8,128)S(1)} collective-permute-done((s32[1032,128]{1,0:T(8,128)S(1)}, s32[1032,128]{1,0:T(8,128)S(1)}, u32[]{:S(2)}, u32[]{:S(2)}) %collective-permute-start.18) | collective-permute-done | bytes 528416 | tf_op jit(solution)/shard_map/ppermute | solution.py:277
  65.7 1.5 %partial_sums.5 = s32[520,128]{1,0:T(8,128)S(1)} custom-call(s32[4,8]{1,0:T(4,128)S(1)} %copy-done.2, f32[2,1024,128]{2,1,0:T(8,128)S(1)} %get-tuple-element.45.kept, s32[1032,128]{1,0:T(8,128)S(1)} %collective-permute-done.18.received, bf16[2,1024,128]{2,1,0:T(8,128)(2,1)S(1)} %collective-permute-done.19.refs_0_, ...), custom_call_target="tpu_custom_call" | custom-call | flops 2097152 | bytes 3940480 | tf_op jit(solution)/shard_map/partial_sums/pallas_call | solution.py:83
  67.2 1.5 %collective-permute-start.24 = (s32[520,128]{1,0:T(8,128)S(1)}, s32[520,128]{1,0:T(8,128)S(1)}, u32[]{:S(2)}, u32[]{:S(2)}) collective-permute-start(s32[520,128]{1,0:T(8,128)S(1)} %partial_sums.5), channel_id=1, source_target_pairs={{0,2},{1,3},{2,4},{3,5},{4,6},{5,7},{6,0},{7,1},{8,10},{9,11},{10,... | collective-permute-start | bytes 798728 | tf_op jit(solution)/shard_map/ppermute | solution.py:280
  68.7 4.0 %collective-permute-done.17.refs_1_ = bf16[2,1024,128]{2,1,0:T(8,128)(2,1)S(1)} collective-permute-done((bf16[2,1024,128]{2,1,0:T(8,128)(2,1)}, bf16[2,1024,128]{2,1,0:T(8,128)(2,1)S(1)}, u32[]{:S(2)}, u32[]{:S(2)}) %collective-permute-start.17) | collective-permute-done | bytes 524320 | tf_op jit(solution)/shard_map/ppermute | solution.py:274
  72.7 8.4 %collective-permute-done.16.refs_1_ = s32[520,128]{1,0:T(8,128)S(1)} collective-permute-done((s32[520,128]{1,0:T(8,128)S(1)}, s32[520,128]{1,0:T(8,128)S(1)}, u32[]{:S(2)}, u32[]{:S(2)}) %collective-permute-start.16) | collective-permute-done | bytes 266272 | tf_op jit(solution)/shard_map/ppermute | solution.py:280
  (43 shorter events, 13.6 us)
Async XLA Ops:
  0.0 15.1 %collective-permute-start = (bf16[1024,256]{1,0:T(8,128)(2,1)}, bf16[1024,256]{1,0:T(8,128)(2,1)S(1)}, u32[]{:S(2)}, u32[]{:S(2)}) collective-permute-start(bf16[1024,256]{1,0:T(8,128)(2,1)} %refs_1_.1), channel_id=1, source_target_pairs={{0,16},{8,24},{16,0},{24,8},{1,17},{9,25},{17,1},{25,9},{2,18},{10... | collective-permute-start | bytes 1572872 | tf_op jit(solution)/shard_map/ppermute | solution.py:274
  2.9 15.5 %collective-permute-start.5 = (bf16[2,1024,128]{2,1,0:T(8,128)(2,1)}, bf16[2,1024,128]{2,1,0:T(8,128)(2,1)S(1)}, u32[]{:S(2)}, u32[]{:S(2)}) collective-permute-start(bf16[2,1024,128]{2,1,0:T(8,128)(2,1)} %refs_2_.1), channel_id=1, source_target_pairs={{0,2},{1,3},{2,4},{3,5},{4,6},{5,7},{6,0},{7,1},{8,10},{9,11},{10,... | collective-permute-start | bytes 1572872 | tf_op jit(solution)/shard_map/ppermute | solution.py:280
  4.5 14.4 %collective-permute-start.1 = (bf16[1024,256]{1,0:T(8,128)(2,1)}, bf16[1024,256]{1,0:T(8,128)(2,1)S(1)}, u32[]{:S(2)}, u32[]{:S(2)}) collective-permute-start(bf16[1024,256]{1,0:T(8,128)(2,1)} %refs_1_.1), channel_id=1, source_target_pairs={{0,8},{8,0},{16,24},{24,16},{1,9},{9,1},{17,25},{25,17},{2,10},{10... | collective-permute-start | bytes 1572872 | tf_op jit(solution)/shard_map/ppermute | solution.py:271
  15.1 11.8 %collective-permute-start.11 = (bf16[2,1024,128]{2,1,0:T(8,128)(2,1)}, bf16[2,1024,128]{2,1,0:T(8,128)(2,1)S(1)}, u32[]{:S(2)}, u32[]{:S(2)}) collective-permute-start(bf16[2,1024,128]{2,1,0:T(8,128)(2,1)} %refs_2_.1), channel_id=1, source_target_pairs={{0,8},{8,0},{16,24},{24,16},{1,9},{9,1},{17,25},{25,17},{2,10},{10... | collective-permute-start | bytes 1572872 | tf_op jit(solution)/shard_map/ppermute | solution.py:271
  18.4 12.5 %collective-permute-start.6 = (bf16[2,1024,128]{2,1,0:T(8,128)(2,1)S(1)}, bf16[2,1024,128]{2,1,0:T(8,128)(2,1)S(1)}, u32[]{:S(2)}, u32[]{:S(2)}) collective-permute-start(bf16[2,1024,128]{2,1,0:T(8,128)(2,1)S(1)} %collective-permute-done.5.refs_0_), channel_id=1, source_target_pairs={{0,16},{8,24},{16,0},{24,8},{1,17},{9,25},{17,1},{25,9},{2,18},{10... | collective-permute-start | bytes 1572872 | tf_op jit(solution)/shard_map/ppermute | solution.py:274
  18.9 14.3 %collective-permute-start.10 = (bf16[2,1024,128]{2,1,0:T(8,128)(2,1)S(1)}, bf16[2,1024,128]{2,1,0:T(8,128)(2,1)S(1)}, u32[]{:S(2)}, u32[]{:S(2)}) collective-permute-start(bf16[2,1024,128]{2,1,0:T(8,128)(2,1)S(1)} %collective-permute-done.5.refs_0_), channel_id=1, source_target_pairs={{0,2},{1,3},{2,4},{3,5},{4,6},{5,7},{6,0},{7,1},{8,10},{9,11},{10,... | collective-permute-start | bytes 1572872 | tf_op jit(solution)/shard_map/ppermute | solution.py:280
  20.5 14.0 %collective-permute-start.3 = (s32[1032,128]{1,0:T(8,128)S(1)}, s32[1032,128]{1,0:T(8,128)S(1)}, u32[]{:S(2)}, u32[]{:S(2)}) collective-permute-start(s32[1032,128]{1,0:T(8,128)S(1)} %get-tuple-element.33), channel_id=1, source_target_pairs={{0,1},{1,0},{2,3},{3,2},{4,5},{5,4},{6,7},{7,6},{8,9},{9,8},{10,11... | collective-permute-start | bytes 1585160 | tf_op jit(solution)/shard_map/ppermute | solution.py:277
  33.2 11.6 %collective-permute-start.12 = (bf16[2,1024,128]{2,1,0:T(8,128)(2,1)S(1)}, bf16[2,1024,128]{2,1,0:T(8,128)(2,1)S(1)}, u32[]{:S(2)}, u32[]{:S(2)}) collective-permute-start(bf16[2,1024,128]{2,1,0:T(8,128)(2,1)S(1)} %collective-permute-done.10.refs_0_), channel_id=1, source_target_pairs={{0,16},{8,24},{16,0},{24,8},{1,17},{9,25},{17,1},{25,9},{2,18},{10... | collective-permute-start | bytes 1572872 | tf_op jit(solution)/shard_map/ppermute | solution.py:274
  34.5 12.9 %collective-permute-start.19 = (bf16[2,1024,128]{2,1,0:T(8,128)(2,1)S(1)}, bf16[2,1024,128]{2,1,0:T(8,128)(2,1)S(1)}, u32[]{:S(2)}, u32[]{:S(2)}) collective-permute-start(bf16[2,1024,128]{2,1,0:T(8,128)(2,1)S(1)} %collective-permute-done.10.refs_0_), channel_id=1, source_target_pairs={{0,2},{1,3},{2,4},{3,5},{4,6},{5,7},{6,0},{7,1},{8,10},{9,11},{10,... | collective-permute-start | bytes 1572872 | tf_op jit(solution)/shard_map/ppermute | solution.py:280
  34.5 16.2 %collective-permute-start.4 = (s32[1032,128]{1,0:T(8,128)S(1)}, s32[1032,128]{1,0:T(8,128)S(1)}, u32[]{:S(2)}, u32[]{:S(2)}) collective-permute-start(s32[1032,128]{1,0:T(8,128)S(1)} %get-tuple-element.34), channel_id=1, source_target_pairs={{0,1},{1,0},{2,3},{3,2},{4,5},{5,4},{6,7},{7,6},{8,9},{9,8},{10,11... | collective-permute-start | bytes 1585160 | tf_op jit(solution)/shard_map/ppermute | solution.py:277
  36.0 12.4 %collective-permute-start.7 = (bf16[2,1024,128]{2,1,0:T(8,128)(2,1)S(1)}, bf16[2,1024,128]{2,1,0:T(8,128)(2,1)S(1)}, u32[]{:S(2)}, u32[]{:S(2)}) collective-permute-start(bf16[2,1024,128]{2,1,0:T(8,128)(2,1)S(1)} %collective-permute-done.5.refs_0_), channel_id=1, source_target_pairs={{0,8},{8,0},{16,24},{24,16},{1,9},{9,1},{17,25},{25,17},{2,10},{10... | collective-permute-start | bytes 1572872 | tf_op jit(solution)/shard_map/ppermute | solution.py:271
  36.0 12.4 %collective-permute-start.8 = (bf16[2,1024,128]{2,1,0:T(8,128)(2,1)S(1)}, bf16[2,1024,128]{2,1,0:T(8,128)(2,1)S(1)}, u32[]{:S(2)}, u32[]{:S(2)}) collective-permute-start(bf16[2,1024,128]{2,1,0:T(8,128)(2,1)S(1)} %collective-permute-done.6.refs_1_), channel_id=1, source_target_pairs={{0,8},{8,0},{16,24},{24,16},{1,9},{9,1},{17,25},{25,17},{2,10},{10... | collective-permute-start | bytes 1572872 | tf_op jit(solution)/shard_map/ppermute | solution.py:271
  47.3 10.1 %collective-permute-start.20 = (bf16[2,1024,128]{2,1,0:T(8,128)(2,1)S(1)}, bf16[2,1024,128]{2,1,0:T(8,128)(2,1)S(1)}, u32[]{:S(2)}, u32[]{:S(2)}) collective-permute-start(bf16[2,1024,128]{2,1,0:T(8,128)(2,1)S(1)} %collective-permute-done.19.refs_0_), channel_id=1, source_target_pairs={{0,16},{8,24},{16,0},{24,8},{1,17},{9,25},{17,1},{25,9},{2,18},{10... | collective-permute-start | bytes 1572872 | tf_op jit(solution)/shard_map/ppermute | solution.py:274
  48.4 9.1 %collective-permute-start.13 = (bf16[2,1024,128]{2,1,0:T(8,128)(2,1)S(1)}, bf16[2,1024,128]{2,1,0:T(8,128)(2,1)S(1)}, u32[]{:S(2)}, u32[]{:S(2)}) collective-permute-start(bf16[2,1024,128]{2,1,0:T(8,128)(2,1)S(1)} %collective-permute-done.10.refs_0_), channel_id=1, source_target_pairs={{0,8},{8,0},{16,24},{24,16},{1,9},{9,1},{17,25},{25,17},{2,10},{10... | collective-permute-start | bytes 1572872 | tf_op jit(solution)/shard_map/ppermute | solution.py:271
  49.9 9.0 %collective-permute-start.9 = (s32[520,128]{1,0:T(8,128)S(1)}, s32[520,128]{1,0:T(8,128)S(1)}, u32[]{:S(2)}, u32[]{:S(2)}) collective-permute-start(s32[520,128]{1,0:T(8,128)S(1)} %partial_sums.3), channel_id=1, source_target_pairs={{0,6},{1,7},{2,0},{3,1},{4,2},{5,3},{6,4},{7,5},{8,14},{9,15},{10,... | collective-permute-start | bytes 798728 | tf_op jit(solution)/shard_map/ppermute | solution.py:280
  50.6 9.3 %collective-permute-start.14 = (bf16[2,1024,128]{2,1,0:T(8,128)(2,1)S(1)}, bf16[2,1024,128]{2,1,0:T(8,128)(2,1)S(1)}, u32[]{:S(2)}, u32[]{:S(2)}) collective-permute-start(bf16[2,1024,128]{2,1,0:T(8,128)(2,1)S(1)} %collective-permute-done.12.refs_1_), channel_id=1, source_target_pairs={{0,8},{8,0},{16,24},{24,16},{1,9},{9,1},{17,25},{25,17},{2,10},{10... | collective-permute-start | bytes 1572872 | tf_op jit(solution)/shard_map/ppermute | solution.py:271
  50.9 14.8 %collective-permute-start.18 = (s32[1032,128]{1,0:T(8,128)S(1)}, s32[1032,128]{1,0:T(8,128)S(1)}, u32[]{:S(2)}, u32[]{:S(2)}) collective-permute-start(s32[1032,128]{1,0:T(8,128)S(1)} %get-tuple-element.46), channel_id=1, source_target_pairs={{0,1},{1,0},{2,3},{3,2},{4,5},{5,4},{6,7},{7,6},{8,9},{9,8},{10,11... | collective-permute-start | bytes 1585160 | tf_op jit(solution)/shard_map/ppermute | solution.py:277
  57.5 4.0 %collective-permute-start.21 = (bf16[2,1024,128]{2,1,0:T(8,128)(2,1)S(1)}, bf16[2,1024,128]{2,1,0:T(8,128)(2,1)S(1)}, u32[]{:S(2)}, u32[]{:S(2)}) collective-permute-start(bf16[2,1024,128]{2,1,0:T(8,128)(2,1)S(1)} %collective-permute-done.19.refs_0_), channel_id=1, source_target_pairs={{0,8},{8,0},{16,24},{24,16},{1,9},{9,1},{17,25},{25,17},{2,10},{10... | collective-permute-start | bytes 1572872 | tf_op jit(solution)/shard_map/ppermute | solution.py:271
  57.5 5.6 %collective-permute-start.22 = (bf16[2,1024,128]{2,1,0:T(8,128)(2,1)S(1)}, bf16[2,1024,128]{2,1,0:T(8,128)(2,1)S(1)}, u32[]{:S(2)}, u32[]{:S(2)}) collective-permute-start(bf16[2,1024,128]{2,1,0:T(8,128)(2,1)S(1)} %collective-permute-done.20.refs_1_), channel_id=1, source_target_pairs={{0,8},{8,0},{16,24},{24,16},{1,9},{9,1},{17,25},{25,17},{2,10},{10... | collective-permute-start | bytes 1572872 | tf_op jit(solution)/shard_map/ppermute | solution.py:271
  58.9 13.8 %collective-permute-start.17 = (bf16[2,1024,128]{2,1,0:T(8,128)(2,1)}, bf16[2,1024,128]{2,1,0:T(8,128)(2,1)S(1)}, u32[]{:S(2)}, u32[]{:S(2)}) collective-permute-start(bf16[2,1024,128]{2,1,0:T(8,128)(2,1)} %refs_2_.1), channel_id=1, source_target_pairs={{0,16},{8,24},{16,0},{24,8},{1,17},{9,25},{17,1},{25,9},{2,18},{10... | collective-permute-start | bytes 1572872 | tf_op jit(solution)/shard_map/ppermute | solution.py:274
  61.4 19.6 %collective-permute-start.16 = (s32[520,128]{1,0:T(8,128)S(1)}, s32[520,128]{1,0:T(8,128)S(1)}, u32[]{:S(2)}, u32[]{:S(2)}) collective-permute-start(s32[520,128]{1,0:T(8,128)S(1)} %partial_sums.4), channel_id=1, source_target_pairs={{0,4},{1,5},{2,6},{3,7},{4,0},{5,1},{6,2},{7,3},{8,12},{9,13},{10,... | collective-permute-start | bytes 798728 | tf_op jit(solution)/shard_map/ppermute | solution.py:280
  61.5 19.8 %collective-permute-start.15 = (s32[1032,128]{1,0:T(8,128)S(1)}, s32[1032,128]{1,0:T(8,128)S(1)}, u32[]{:S(2)}, u32[]{:S(2)}) collective-permute-start(s32[1032,128]{1,0:T(8,128)S(1)} %get-tuple-element.42), channel_id=1, source_target_pairs={{0,1},{1,0},{2,3},{3,2},{4,5},{5,4},{6,7},{7,6},{8,9},{9,8},{10,11... | collective-permute-start | bytes 1585160 | tf_op jit(solution)/shard_map/ppermute | solution.py:277
  67.2 15.4 %collective-permute-start.24 = (s32[520,128]{1,0:T(8,128)S(1)}, s32[520,128]{1,0:T(8,128)S(1)}, u32[]{:S(2)}, u32[]{:S(2)}) collective-permute-start(s32[520,128]{1,0:T(8,128)S(1)} %partial_sums.5), channel_id=1, source_target_pairs={{0,2},{1,3},{2,4},{3,5},{4,6},{5,7},{6,0},{7,1},{8,10},{9,11},{10,... | collective-permute-start | bytes 798728 | tf_op jit(solution)/shard_map/ppermute | solution.py:280
  72.7 8.6 %collective-permute-start.23 = (bf16[2,1024,128]{2,1,0:T(8,128)(2,1)S(1)}, bf16[2,1024,128]{2,1,0:T(8,128)(2,1)S(1)}, u32[]{:S(2)}, u32[]{:S(2)}) collective-permute-start(bf16[2,1024,128]{2,1,0:T(8,128)(2,1)S(1)} %collective-permute-done.17.refs_1_), channel_id=1, source_target_pairs={{0,8},{8,0},{16,24},{24,16},{1,9},{9,1},{17,25},{25,17},{2,10},{10... | collective-permute-start | bytes 1572872 | tf_op jit(solution)/shard_map/ppermute | solution.py:271
  (4 other events, 30.2 us)
